TPU v7x, 32 devices: a whole 2x2x4 slice. The times are simulated.
32 devices in a mesh: groups: 2 (over x), ctx: 8 (over z, y), width: 2 (over core).
Axes of the slice: x: 2, y: 2, z: 4, core: 2. Of those that a mesh axis runs over, the one named last changes fastest.
Arguments:
- gating_vectors: bfloat16 [2048, 4096], P(('groups', 'ctx'), 'width'), parts along dimension 0, may hold values from -3 to 3
- lookup_vectors: bfloat16 [2048, 4096], P(('groups', 'ctx'), 'width'), parts along dimension 0, may hold values from -3 to 3
- payload_vectors: bfloat16 [2048, 4096], P(('groups', 'ctx'), 'width'), parts along dimension 0, may hold values from -6 to 6
- forgetting_exponent: bfloat16 [2048, 4096], P(('groups', 'ctx'), 'width'), parts along dimension 0, may hold values from 0 to 0.5
- inline_adapt_factor: bfloat16 [2048, 4096], P(('groups', 'ctx'), 'width'), parts along dimension 0, may hold values from 0 to 0.9
- group_layer_scaling: float32 [4096], P('width'), may hold values from 0.5 to 1.5
- group_layer_offset: float32 [4096], P('width'), may hold values from -3 to 3
- present_reward_factor: float32 [4096], P('width'), may hold values from -1 to 1
- shared_dictionary_matrix: bfloat16 [16384, 4096], P('ctx', 'width'), may hold values from -0.09375 to 0.09375
- sparse_code_offset: float32 [16384], P('ctx'), may hold values from -3 to 3
- reconstruct_offset: float32 [4096], P('width'), may hold values from -2 to 2
- panel_holder_choice: int32 [256, 2], P(('groups', 'ctx')), parts along dimension 0, may hold values from 0 to 7, all different within a row; in each aligned block of 16 rows (0 to 15, 16 to 31, ...) at most 8 rows name the same one
- holder_group_enabled: int32 [256, 2, 16], P(('groups', 'ctx')), parts along dimension 0, may hold values 0 or 1
- fixed_feature_slot: int32 [128], P('ctx'), may hold values from 0 to 127
- fixed_feature_amount: float32 [128], P('ctx'), may hold values from 2 to 8
Outputs:
- standardized_mixer_result: bfloat16 [2048, 4096], P(('groups', 'ctx'), 'width'), parts along dimension 0
- steered: bfloat16 [2048, 4096], P(('groups', 'ctx'), 'width'), parts along dimension 0
There are 2 independent parts, one for each index of `groups`. A program takes and returns all parts, laid end to end along the dimension named above; an argument that names none is the same for every part. Nothing has to cross between parts.
Inputs may be any that keep to these rules, and one draw needn't show every extreme that they name: `panel_holder_choice`: each tile names 2 different owners; the tiles of one device name one owner at most 8 times, and in every draw some device's tiles name some owner exactly 8 times.
All inputs are finite; a program needn't handle non-finite values. No bound on the sum of `holder_group_enabled` on one device may be relied on, other than what follows from the above.
Results may differ from a plain program's by a relative error of at most 0.015.
Values may be sent and summed in bfloat16 or wider, within the bound.
A program may use at most 128 MiB of HBM per device.

v0:
```python
import jax
import jax.numpy as jnp
from jax import lax
from jax.sharding import PartitionSpec as P

ATTN_GROUP_DIM = 64
SUB = 32
TILE = 8
BLK = 128


HIGHEST = lax.Precision.HIGHEST


def passed_along(block, axis, distance):
    devices = range(lax.axis_size(axis))
    route = [(i - distance, i) for i in devices if i - distance in devices]
    return lax.ppermute(block, axis, route)


def block_step(carried, pieces):
    rec_in, key_in, val_in, rate_in, learn_in = pieces
    length = rec_in.shape[0]
    removal = key_in * lax.rsqrt(
        jnp.sum(key_in * key_in, -1, keepdims=True) + key_in.shape[-1] * 1e-05
    )
    erase_a = -removal
    erase_b = removal * learn_in
    log_cum = -jnp.cumsum(rate_in, axis=0)
    cum_now = jnp.exp(log_cum)
    cum_prev = jnp.exp(log_cum + rate_in)
    undo = jnp.exp(-log_cum)
    left_a = erase_a * cum_prev
    left_r = rec_in * cum_now
    right_b = erase_b * undo
    right_k = key_in * undo
    row_ids = lax.broadcasted_iota(jnp.int32, (length, length), 0)
    col_ids = lax.broadcasted_iota(jnp.int32, (length, length), 1)
    strict = (row_ids > col_ids).astype(jnp.float32)
    inclusive = (row_ids >= col_ids).astype(jnp.float32)
    mix_ab = jnp.einsum("thk,jhk->htj", left_a, right_b, precision=HIGHEST) * strict
    mix_ak = jnp.einsum("thk,jhk->htj", left_a, right_k, precision=HIGHEST) * strict
    mix_rb = jnp.einsum("thk,jhk->htj", left_r, right_b, precision=HIGHEST) * inclusive
    mix_rk = jnp.einsum("thk,jhk->htj", left_r, right_k, precision=HIGHEST) * inclusive
    padded_v = jnp.concatenate([val_in, jnp.zeros_like(val_in)], -1)
    target = jnp.einsum("thk,hxk->htx", left_a, carried, precision=HIGHEST) + jnp.einsum(
        "htj,jhx->htx", mix_ak, padded_v, precision=HIGHEST
    )
    inverse = jnp.eye(length, dtype=jnp.float32)[None] + mix_ab
    power = mix_ab
    for doubling in range(length.bit_length() - 2):
        power = jnp.einsum("hij,hjk->hik", power, power, precision=HIGHEST)
        inverse = inverse + jnp.einsum("hij,hjk->hik", inverse, power, precision=HIGHEST)
    reads = jnp.einsum("htj,hjx->htx", inverse, target, precision=HIGHEST)
    outputs = (
        jnp.einsum("thk,hxk->htx", left_r, carried, precision=HIGHEST)
        + jnp.einsum("htj,hjx->htx", mix_rb, reads, precision=HIGHEST)
        + jnp.einsum("htj,jhx->htx", mix_rk, padded_v, precision=HIGHEST)
    )
    fade = cum_now[-1]
    updated = (
        carried
        + jnp.einsum("hjx,jhk->hxk", reads, right_b, precision=HIGHEST)
        + jnp.einsum("jhx,jhk->hxk", padded_v, right_k, precision=HIGHEST)
    )
    return (updated * fade[:, None, :], outputs)


def activate(preacts, mask_vals, index_vals, value_vals):
    senders, items, block_count = mask_vals.shape
    codes = jnp.maximum(preacts, 0.0).reshape(senders, items, TILE, block_count, BLK)
    within = lax.broadcasted_iota(jnp.int32, (block_count, BLK), 1)
    hit = within == index_vals[:, None]
    codes = jnp.where(hit, value_vals[:, None], codes)
    codes = codes * mask_vals.astype(jnp.float32)[:, :, None, :, None]
    return codes.reshape(senders * items * TILE, block_count * BLK).astype(jnp.bfloat16)


def body(
    gating_vectors,
    lookup_vectors,
    payload_vectors,
    forgetting_exponent,
    inline_adapt_factor,
    group_layer_scaling,
    group_layer_offset,
    present_reward_factor,
    shared_dictionary_matrix,
    sparse_code_offset,
    reconstruct_offset,
    panel_holder_choice,
    holder_group_enabled,
    fixed_feature_slot,
    fixed_feature_amount,
):
    tok_rows = gating_vectors.shape[0]
    feat_local = gating_vectors.shape[1]
    group_counting = feat_local // ATTN_GROUP_DIM
    gating_vectors_all = gating_vectors.astype(jnp.float32).reshape(
        tok_rows, group_counting, ATTN_GROUP_DIM
    )
    lookup_vectors_all = lookup_vectors.astype(jnp.float32).reshape(
        tok_rows, group_counting, ATTN_GROUP_DIM
    )
    payload_vectors_all = payload_vectors.astype(jnp.float32).reshape(
        tok_rows, group_counting, ATTN_GROUP_DIM
    )
    rate_all = forgetting_exponent.astype(jnp.float32).reshape(
        tok_rows, group_counting, ATTN_GROUP_DIM
    )
    learn_all = inline_adapt_factor.astype(jnp.float32).reshape(
        tok_rows, group_counting, ATTN_GROUP_DIM
    )
    block_count = tok_rows // SUB

    def stacked(array):
        return array.reshape(block_count, SUB, group_counting, ATTN_GROUP_DIM)

    eye_heads = jnp.broadcast_to(
        jnp.eye(ATTN_GROUP_DIM, dtype=jnp.float32), (group_counting, ATTN_GROUP_DIM, ATTN_GROUP_DIM)
    )
    zero_heads = jnp.zeros((group_counting, ATTN_GROUP_DIM, ATTN_GROUP_DIM), jnp.float32)
    start_state = jnp.concatenate([zero_heads, eye_heads], axis=1)
    final_state, block_outs = lax.scan(
        block_step,
        start_state,
        (
            stacked(gating_vectors_all),
            stacked(lookup_vectors_all),
            stacked(payload_vectors_all),
            stacked(rate_all),
            stacked(learn_all),
        ),
    )
    block_outs = block_outs.transpose(0, 2, 1, 3).reshape(
        tok_rows, group_counting, 2 * ATTN_GROUP_DIM
    )
    local_out = block_outs[:, :, :ATTN_GROUP_DIM]
    probe = block_outs[:, :, ATTN_GROUP_DIM:]
    own_state = final_state[:, :ATTN_GROUP_DIM, :]
    transfer = final_state[:, ATTN_GROUP_DIM:, :]

    def forward(counter, carry_pair):
        incoming = passed_along(carry_pair[1], "ctx", 1)
        leaving = jnp.einsum("hvj,hjk->hvk", incoming, transfer, precision=HIGHEST) + own_state
        return (incoming, leaving)

    prior = lax.fori_loop(0, lax.axis_size("ctx") - 1, forward, (zero_heads, own_state))[0]
    wkv = local_out + jnp.einsum("hvk,thk->thv", prior, probe, precision=HIGHEST)
    center = wkv - jnp.mean(wkv, -1, keepdims=True)
    spread = jnp.mean(center * center, -1, keepdims=True)
    standardized_lines = (center * lax.rsqrt(spread + 1e-05)).reshape(
        tok_rows, feat_local
    ) * group_layer_scaling + group_layer_offset
    present_reward = (
        jnp.sum(
            gating_vectors_all
            * lookup_vectors_all
            * present_reward_factor.reshape(group_counting, ATTN_GROUP_DIM),
            -1,
            keepdims=True,
        )
        * payload_vectors_all
    ).reshape(tok_rows, feat_local)
    standardized_mixer_result = (standardized_lines + present_reward).astype(jnp.bfloat16)
    enc_in = (standardized_mixer_result.astype(jnp.float32) - reconstruct_offset).astype(
        jnp.bfloat16
    )
    ctx_count = lax.axis_size("ctx")
    tile_count = tok_rows // TILE
    slot_count = panel_holder_choice.shape[1]
    blocks_own = holder_group_enabled.shape[2]
    capacity = max(2, 2 * tok_rows * slot_count // (TILE * ctx_count))
    pair_count = tile_count * slot_count
    owner_flat = panel_holder_choice.reshape(pair_count)
    owner_hot = (owner_flat[:, None] == lax.broadcasted_iota(jnp.int32, (1, ctx_count), 1)).astype(
        jnp.int32
    )
    ranks = jnp.sum((jnp.cumsum(owner_hot, axis=0) - owner_hot) * owner_hot, axis=1)
    slot_ids = owner_flat * capacity + ranks
    dispatch = (
        slot_ids[None, :] == lax.broadcasted_iota(jnp.int32, (ctx_count * capacity, 1), 0)
    ).astype(jnp.float32)
    tile_pick = (
        lax.broadcasted_iota(jnp.int32, (tile_count, pair_count), 1) // slot_count
        == lax.broadcasted_iota(jnp.int32, (tile_count, pair_count), 0)
    ).astype(jnp.float32)
    slot_tile = jnp.dot(dispatch, tile_pick.T)
    send_rows = jnp.dot(
        slot_tile.astype(jnp.bfloat16),
        enc_in.reshape(tile_count, TILE * feat_local),
        preferred_element_type=jnp.float32,
    )
    send_rows = send_rows.astype(jnp.bfloat16).reshape(ctx_count, capacity, TILE, feat_local)
    send_mask = jnp.dot(
        dispatch, holder_group_enabled.reshape(pair_count, blocks_own).astype(jnp.float32)
    )
    send_mask = send_mask.astype(jnp.bfloat16).reshape(ctx_count, capacity, blocks_own)
    got_rows = lax.all_to_all(send_rows, "ctx", split_axis=0, concat_axis=0, tiled=True)
    got_mask = lax.all_to_all(send_mask, "ctx", split_axis=0, concat_axis=0, tiled=True)
    senders = got_rows.shape[0]
    items = got_rows.shape[1]
    flat_rows = got_rows.reshape(senders * items * TILE, feat_local)
    partial_pre = lax.dot_general(
        flat_rows,
        shared_dictionary_matrix,
        (((1,), (1,)), ((), ())),
        preferred_element_type=jnp.float32,
    )
    total_pre = lax.psum(partial_pre.astype(jnp.bfloat16), "width").astype(jnp.float32)
    codes = activate(
        total_pre + sparse_code_offset, got_mask, fixed_feature_slot, fixed_feature_amount
    )
    decoded = jnp.dot(codes, shared_dictionary_matrix, preferred_element_type=jnp.float32).astype(
        jnp.bfloat16
    )
    returned = decoded.reshape(senders, items, TILE, feat_local)
    received = lax.all_to_all(returned, "ctx", split_axis=0, concat_axis=0, tiled=True)
    summed = jnp.dot(
        slot_tile.T.astype(jnp.bfloat16),
        received.reshape(ctx_count * capacity, TILE * feat_local),
        preferred_element_type=jnp.float32,
    )
    steered = (summed.reshape(tok_rows, feat_local) + reconstruct_offset).astype(jnp.bfloat16)
    return (standardized_mixer_result, steered)


def solution(mesh):
    placed = (
        P(("groups", "ctx"), "width"),
        P(("groups", "ctx"), "width"),
        P(("groups", "ctx"), "width"),
        P(("groups", "ctx"), "width"),
        P(("groups", "ctx"), "width"),
        P("width"),
        P("width"),
        P("width"),
        P("ctx", "width"),
        P("ctx"),
        P("width"),
        P(("groups", "ctx"), None),
        P(("groups", "ctx"), None, None),
        P("ctx"),
        P("ctx"),
    )
    return jax.shard_map(
        body,
        mesh=mesh,
        in_specs=placed,
        out_specs=(P(("groups", "ctx"), "width"), P(("groups", "ctx"), "width")),
        check_vma=False,
    )
```

profile of v0, /device:TPU:1, one launch (start us, length us, event | category | flops | bytes accessed | tf_op | source)
XLA Modules:
  0.0 517.8 jit_solution(18060309378639857099)
XLA Ops:
  14.9 3.0 reshape_reshape.26
  17.9 3.1 reshape_reshape.27
  21.0 2.3 reshape.120
  23.3 2.3 reshape.121
  26.0 119.1 %while.24 = (s32[]{:T(128)}, f32[32,128,64]{1,2,0:T(8,128)S(1)}, f32[4,32,32,128]{3,1,2,0:T(8,128)}, f32[4,32,32,64]{3,2,1,0:T(8,128)S(1)}, f32[4,32,32,64]{3,2,...) while((s32[]{:T(128)}, f32[32,128,64]{1,2,0:T(8,128)S(1)}, ...), condition=%wide.region_3.4_spmd, body=%wide.region_0.3_spmd.sunk | while | flops 809539584 | bytes 26289764 | solution.py:124
  56.1 2.0 convolution_add_fusion.21
  64.0 2.2 fusion.214
  82.1 2.0 convolution_add_fusion.21
  90.0 2.2 fusion.214
  108.0 2.0 convolution_add_fusion.21
  115.9 2.2 fusion.214
  119.4 2.0 bitcast_multiply_fusion.8
  134.0 2.0 convolution_add_fusion.21
  141.9 2.2 fusion.214
  149.7 4.8 fusion.64
  154.6 3.6 copy.85
  158.2 182.7 %while.25 = (s32[]{:T(128)}, f32[32,64,64]{2,1,0:T(8,128)}, f32[32,64,64]{2,1,0:T(8,128)}, f32[32,64,64]{2,1,0:T(8,128)S(1)}, f32[32,64,64]{2,1,0:T(8,128)S(1)}, /*index=5*/s32[]{:T(128)}) while((s32[]{:T(128)}, f32[32,64,64]{2,1,0:T(8,128)}, f32[32,64,64]{2,1,0:T(8,128)}, f32[32,64,64]{2,1,0:T(8,128)S(1)}, f32[32,64,64]{2,1,0:T(8,128)S(1)}, ...), condition=%wide.region_5.6_spmd, body=%wide.region_4.5_spmd.sunk | while | flops 100794368 | bytes 6291593 | solution.py:148
  158.2 4.0 collective-permute-start
  162.2 22.1 %collective-permute-done = f32[32,64,64]{2,1,0:T(8,128)S(1)} collective-permute-done((f32[32,64,64]{2,1,0:T(8,128)}, f32[32,64,64]{2,1,0:T(8,128)S(1)}, u32[]{:S(2)}, u32[]{:S(2)}) %collective-permute-start) | collective-permute-done | bytes 524320 | tf_op jit(solution)/shard_map/while/body/eval_jaxpr/ppermute | solution.py:18
  184.3 2.2 convolution_add_fusion.22
  186.5 4.1 collective-permute-start
  190.6 21.1 %collective-permute-done = f32[32,64,64]{2,1,0:T(8,128)S(1)} collective-permute-done((f32[32,64,64]{2,1,0:T(8,128)}, f32[32,64,64]{2,1,0:T(8,128)S(1)}, u32[]{:S(2)}, u32[]{:S(2)}) %collective-permute-start) | collective-permute-done | bytes 524320 | tf_op jit(solution)/shard_map/while/body/eval_jaxpr/ppermute | solution.py:18
  211.7 2.2 convolution_add_fusion.22
  214.0 4.1 collective-permute-start
  218.1 20.2 %collective-permute-done = f32[32,64,64]{2,1,0:T(8,128)S(1)} collective-permute-done((f32[32,64,64]{2,1,0:T(8,128)}, f32[32,64,64]{2,1,0:T(8,128)S(1)}, u32[]{:S(2)}, u32[]{:S(2)}) %collective-permute-start) | collective-permute-done | bytes 524320 | tf_op jit(solution)/shard_map/while/body/eval_jaxpr/ppermute | solution.py:18
  238.3 2.2 convolution_add_fusion.22
  240.5 5.0 collective-permute-start
  245.5 19.3 %collective-permute-done = f32[32,64,64]{2,1,0:T(8,128)S(1)} collective-permute-done((f32[32,64,64]{2,1,0:T(8,128)}, f32[32,64,64]{2,1,0:T(8,128)S(1)}, u32[]{:S(2)}, u32[]{:S(2)}) %collective-permute-start) | collective-permute-done | bytes 524320 | tf_op jit(solution)/shard_map/while/body/eval_jaxpr/ppermute | solution.py:18
  264.7 2.2 convolution_add_fusion.22
  267.0 5.0 collective-permute-start
  271.9 18.4 %collective-permute-done = f32[32,64,64]{2,1,0:T(8,128)S(1)} collective-permute-done((f32[32,64,64]{2,1,0:T(8,128)}, f32[32,64,64]{2,1,0:T(8,128)S(1)}, u32[]{:S(2)}, u32[]{:S(2)}) %collective-permute-start) | collective-permute-done | bytes 524320 | tf_op jit(solution)/shard_map/while/body/eval_jaxpr/ppermute | solution.py:18
  290.3 2.2 convolution_add_fusion.22
  292.5 5.0 collective-permute-start
  297.5 17.4 %collective-permute-done = f32[32,64,64]{2,1,0:T(8,128)S(1)} collective-permute-done((f32[32,64,64]{2,1,0:T(8,128)}, f32[32,64,64]{2,1,0:T(8,128)S(1)}, u32[]{:S(2)}, u32[]{:S(2)}) %collective-permute-start) | collective-permute-done | bytes 524320 | tf_op jit(solution)/shard_map/while/body/eval_jaxpr/ppermute | solution.py:18
  314.9 2.2 convolution_add_fusion.22
  317.2 5.0 collective-permute-start
  322.1 16.5 %collective-permute-done = f32[32,64,64]{2,1,0:T(8,128)S(1)} collective-permute-done((f32[32,64,64]{2,1,0:T(8,128)}, f32[32,64,64]{2,1,0:T(8,128)S(1)}, u32[]{:S(2)}, u32[]{:S(2)}) %collective-permute-start) | collective-permute-done | bytes 524320 | tf_op jit(solution)/shard_map/while/body/eval_jaxpr/ppermute | solution.py:18
  338.7 2.2 convolution_add_fusion.22
  340.9 7.0 %fusion.66 = (f32[128,32]{0,1:T(8,128)S(1)}, f32[128,32,64]{0,2,1:T(8,128)S(1)}) fusion(f32[128,32,64]{0,2,1:T(8,128)} %copy.85, f32[32,64,64]{2,1,0:T(8,128)} %get-tuple-element.73, f32[128,32,64]{2,1,0:T(8,128)} %get-tuple-element.138), kind=kOutput, calls=%fused_computation.118 | convolution fusion | flops 201846784 | bytes 3686400 | tf_op jit(solution)/shard_map/hvk,thk->thv/dot_general | solution.py:149
  349.1 2.9 fusion.36
  356.4 53.4 %all_to_all.15 = bf16[8,8,8,2048]{3,2,1,0:T(8,128)(2,1)S(1)} all-to-all(bf16[8,8,8,2048]{3,2,1,0:T(8,128)(2,1)S(1)} %copy.77), channel_id=1, replica_groups=mesh['groups'=2,'ctx'=8,'width'=2] {'ctx'}, dimensions={0} | all-to-all | bytes 4194304 | tf_op jit(solution)/shard_map/all_to_all | solution.py:199
  409.8 9.1 %convolution_convert_fusion.2 = bf16[512,2048]{1,0:T(8,128)(2,1)} fusion(bf16[512,2048]{1,0:T(8,128)(2,1)S(1)} %bitcast.176, bf16[2048,2048]{1,0:T(8,128)(2,1)} %param.27), kind=kOutput, calls=%fused_computation.68 | convolution fusion | flops 4296015872 | bytes 12582912 | tf_op jit(solution)/shard_map/dot_general | solution.py:204
  420.6 3.9 all-to-all-start.1
  424.7 5.3 %all-to-all-done.1 = bf16[8,8,16]{2,1,0:T(8,128)(2,1)S(1)} async-done(((bf16[8,8,16]{2,1,0:T(8,128)(2,1)}), bf16[8,8,16]{2,1,0:T(8,128)(2,1)S(1)}, u32[]{:S(2)}, u32[]{:S(2)}) %all-to-all-start.1) | async-done | bytes 2080 | tf_op jit(solution)/shard_map/all_to_all | solution.py:200
  429.9 13.1 %all-reduce.4.cloned.1.call-done = bf16[512,2048]{1,0:T(8,128)(2,1)} async-done(((bf16[512,2048]{1,0:T(8,128)(2,1)}), bf16[512,2048]{1,0:T(8,128)(2,1)}) %all-reduce.4.cloned.1.call-update) | async-done | bytes 2097168 | tf_op jit(solution)/shard_map/psum | solution.py:210
  444.6 9.2 %convolution_convert_fusion.1 = bf16[512,2048]{1,0:T(8,128)(2,1)} fusion(bf16[2048,2048]{1,0:T(8,128)(2,1)} %param.27, f32[512,2048]{1,0:T(8,128)S(1)} %bitcast.173, bf16[512,2048]{1,0:T(8,128)(2,1)S(1)} %copy-done.15, f32[2048]{0:T(1024)S(1)} %copy-done.16, f32[2048]{0:T(1024)S(1)} %broadcast_bitcast_fusion, pred[2048]{0:T(1024)(128)(4,1)S(1)} %fusion.58), kind=kOutput, calls=%fused_computation.67 | convolution fusion | flops 4302307328 | bytes 16795648 | tf_op jit(solution)/shard_map/dot_general | solution.py:214
  453.8 5.6 %all-to-all-start.2 = ((bf16[8,8,8,2048]{3,2,1,0:T(8,128)(2,1)}), bf16[8,8,8,2048]{3,2,1,0:T(8,128)(2,1)S(1)}, u32[]{:S(2)}, u32[]{:S(2)}) async-start(bf16[8,8,8,2048]{3,2,1,0:T(8,128)(2,1)} %bitcast.175), calls=%async_computation.2 | async-start | bytes 4194304 | tf_op jit(solution)/shard_map/all_to_all | solution.py:218
  460.4 46.8 %all-to-all-done.2 = bf16[8,8,8,2048]{3,2,1,0:T(8,128)(2,1)S(1)} async-done(((bf16[8,8,8,2048]{3,2,1,0:T(8,128)(2,1)}), bf16[8,8,8,2048]{3,2,1,0:T(8,128)(2,1)S(1)}, u32[]{:S(2)}, u32[]{:S(2)}) %all-to-all-start.2) | async-done | bytes 2097184 | tf_op jit(solution)/shard_map/all_to_all | solution.py:218
  (207 shorter events, 110.5 us)
Async XLA Ops:
  7.2 417.3 %copy-start = (f32[16]{0:T(128)S(1)}, f32[16]{0:T(128)}, u32[]{:S(2)}) copy-start(f32[16]{0:T(128)} %param.33) | copy-start | bytes 196
  7.2 1.7 copy-start.7
  7.2 435.8 %all-reduce.4.cloned.1.call-start = ((), (), s32[]{:S(2)}) async-start(), calls=%async_computation.3 | async-start | bytes 4194304 | tf_op jit(solution)/shard_map/psum | solution.py:210
  13.6 4.3 copy-start.2
  17.9 3.1 copy-start.5
  21.0 2.3 copy-start.6
  158.2 26.1 %collective-permute-start = (f32[32,64,64]{2,1,0:T(8,128)}, f32[32,64,64]{2,1,0:T(8,128)S(1)}, u32[]{:S(2)}, u32[]{:S(2)}) collective-permute-start(f32[32,64,64]{2,1,0:T(8,128)} %get-tuple-element.269), channel_id=1, source_target_pairs={{0,2},{2,4},{4,6},{6,8},{8,10},{10,12},{12,14},{1,3},{3,5},{5,7},{... | collective-permute-start | bytes 1572872 | tf_op jit(solution)/shard_map/while/body/eval_jaxpr/ppermute | solution.py:18
  184.3 2.2 copy-start.1
  186.5 25.2 %collective-permute-start = (f32[32,64,64]{2,1,0:T(8,128)}, f32[32,64,64]{2,1,0:T(8,128)S(1)}, u32[]{:S(2)}, u32[]{:S(2)}) collective-permute-start(f32[32,64,64]{2,1,0:T(8,128)} %get-tuple-element.269), channel_id=1, source_target_pairs={{0,2},{2,4},{4,6},{6,8},{8,10},{10,12},{12,14},{1,3},{3,5},{5,7},{... | collective-permute-start | bytes 1572872 | tf_op jit(solution)/shard_map/while/body/eval_jaxpr/ppermute | solution.py:18
  211.7 2.2 copy-start.1
  214.0 24.3 %collective-permute-start = (f32[32,64,64]{2,1,0:T(8,128)}, f32[32,64,64]{2,1,0:T(8,128)S(1)}, u32[]{:S(2)}, u32[]{:S(2)}) collective-permute-start(f32[32,64,64]{2,1,0:T(8,128)} %get-tuple-element.269), channel_id=1, source_target_pairs={{0,2},{2,4},{4,6},{6,8},{8,10},{10,12},{12,14},{1,3},{3,5},{5,7},{... | collective-permute-start | bytes 1572872 | tf_op jit(solution)/shard_map/while/body/eval_jaxpr/ppermute | solution.py:18
  238.3 2.2 copy-start.1
  240.5 24.2 %collective-permute-start = (f32[32,64,64]{2,1,0:T(8,128)}, f32[32,64,64]{2,1,0:T(8,128)S(1)}, u32[]{:S(2)}, u32[]{:S(2)}) collective-permute-start(f32[32,64,64]{2,1,0:T(8,128)} %get-tuple-element.269), channel_id=1, source_target_pairs={{0,2},{2,4},{4,6},{6,8},{8,10},{10,12},{12,14},{1,3},{3,5},{5,7},{... | collective-permute-start | bytes 1572872 | tf_op jit(solution)/shard_map/while/body/eval_jaxpr/ppermute | solution.py:18
  264.7 2.2 copy-start.1
  267.0 23.3 %collective-permute-start = (f32[32,64,64]{2,1,0:T(8,128)}, f32[32,64,64]{2,1,0:T(8,128)S(1)}, u32[]{:S(2)}, u32[]{:S(2)}) collective-permute-start(f32[32,64,64]{2,1,0:T(8,128)} %get-tuple-element.269), channel_id=1, source_target_pairs={{0,2},{2,4},{4,6},{6,8},{8,10},{10,12},{12,14},{1,3},{3,5},{5,7},{... | collective-permute-start | bytes 1572872 | tf_op jit(solution)/shard_map/while/body/eval_jaxpr/ppermute | solution.py:18
  290.3 2.2 copy-start.1
  292.5 22.4 %collective-permute-start = (f32[32,64,64]{2,1,0:T(8,128)}, f32[32,64,64]{2,1,0:T(8,128)S(1)}, u32[]{:S(2)}, u32[]{:S(2)}) collective-permute-start(f32[32,64,64]{2,1,0:T(8,128)} %get-tuple-element.269), channel_id=1, source_target_pairs={{0,2},{2,4},{4,6},{6,8},{8,10},{10,12},{12,14},{1,3},{3,5},{5,7},{... | collective-permute-start | bytes 1572872 | tf_op jit(solution)/shard_map/while/body/eval_jaxpr/ppermute | solution.py:18
  314.9 2.2 copy-start.1
  317.2 21.5 %collective-permute-start = (f32[32,64,64]{2,1,0:T(8,128)}, f32[32,64,64]{2,1,0:T(8,128)S(1)}, u32[]{:S(2)}, u32[]{:S(2)}) collective-permute-start(f32[32,64,64]{2,1,0:T(8,128)} %get-tuple-element.269), channel_id=1, source_target_pairs={{0,2},{2,4},{4,6},{6,8},{8,10},{10,12},{12,14},{1,3},{3,5},{5,7},{... | collective-permute-start | bytes 1572872 | tf_op jit(solution)/shard_map/while/body/eval_jaxpr/ppermute | solution.py:18
  338.6 2.2 copy-start.1
  347.8 0.7 copy-start.12
  347.9 1.2 copy-start.4
  348.1 3.9 copy-start.3
  348.1 3.9 copy-start.8
  348.1 3.9 copy-start.10
  348.1 3.9 copy-start.11
  352.1 1.6 copy-start.13
  418.9 0.7 copy-start.9
  418.9 5.6 %copy-start.14 = (s32[16]{0:T(128)S(1)}, s32[16]{0:T(128)}, u32[]{:S(2)}) copy-start(s32[16]{0:T(128)} %param.32) | copy-start | bytes 196
  420.6 9.4 %all-to-all-start.1 = ((bf16[8,8,16]{2,1,0:T(8,128)(2,1)}), bf16[8,8,16]{2,1,0:T(8,128)(2,1)S(1)}, u32[]{:S(2)}, u32[]{:S(2)}) async-start(bf16[8,8,16]{2,1,0:T(8,128)(2,1)} %bitcast.19), calls=%async_computation.1 | async-start | bytes 32768 | tf_op jit(solution)/shard_map/all_to_all | solution.py:200
  424.7 19.5 %copy-start.16 = (f32[2048]{0:T(1024)S(1)}, f32[2048]{0:T(1024)}, u32[]{:S(2)}) copy-start(f32[2048]{0:T(1024)} %param.28) | copy-start | bytes 24580
  443.0 1.6 copy-start.15
  453.8 53.4 %all-to-all-start.2 = ((bf16[8,8,8,2048]{3,2,1,0:T(8,128)(2,1)}), bf16[8,8,8,2048]{3,2,1,0:T(8,128)(2,1)S(1)}, u32[]{:S(2)}, u32[]{:S(2)}) async-start(bf16[8,8,8,2048]{3,2,1,0:T(8,128)(2,1)} %bitcast.175), calls=%async_computation.2 | async-start | bytes 4194304 | tf_op jit(solution)/shard_map/all_to_all | solution.py:218
Sparse Core Ops, SparseCore 0:
  419.1 23.8 all-reduce.3
where the time goes:
time: 525 us; the launch traced here: 518 us
  waiting for transfers between devices  200 us (38%)
  matrix products  127 us (24%)
  blocking collectives  53.4 us (10%)
  local copies, waits for them, and re-layouts  50.3 us (10%)
  starting transfers between devices  41.5 us (8%)
  loops' own time  16.2 us (3%)
  other arithmetic  15 us (3%)
  between operations  14.6 us (3%)
    ppermute x7, waiting for transfers between devices, passed_along(): return lax.ppermute(block, axis, route)  135 us
    all_to_all x1, blocking collectives, body(): lax.all_to_all(send_rows, 'ctx', split_axis=0, concat_axis=0, tiled=True)  53.4 us
    all_to_all x1, waiting for transfers between devices, body(): lax.all_to_all(returned, 'ctx', split_axis=0, concat_axis=0, tiled=True)  46.8 us
    ppermute x7, starting transfers between devices, passed_along(): return lax.ppermute(block, axis, route)  32 us
    another operation x1, loops' own time, body(): lax.scan(block_step, start_state, (stacked(gating_vectors_all), stacked(l...  16.1 us
    dot_general x7, matrix products, forward(): jnp.einsum('hvj,hjk->hvk', incoming, transfer, precision=HIGHEST)  15.6 us
    psum x1, waiting for transfers between devices, body(): lax.psum(partial_pre.astype(jnp.bfloat16), 'width').astype(jnp.float32)  13.1 us
    unnamed x41, local copies, waits for them, and re-layouts  12.8 us
  transfers between devices with their start and end apart: 10, of which 10 were waited for; matrix products, arithmetic and copies ran while one was open for 0% of the time, Pallas kernels for 0%

commit v1 on v0

v1 whole, which is shorter than its diff:
```python
import functools

import jax
import jax.numpy as jnp
from jax import lax
from jax.experimental import pallas as pl
from jax.experimental.pallas import tpu as pltpu
from jax.sharding import PartitionSpec as P

ATTN_GROUP_DIM = 64
TILE = 8
BLK = 128
LANES = 128
PAIRS = 2

HIGHEST = lax.Precision.HIGHEST
BF16 = jnp.bfloat16
F32 = jnp.float32
ROWS_COLS = (((1,), (0,)), ((), ()))
COLS_COLS = (((1,), (1,)), ((), ()))
ROWS_ROWS = (((0,), (0,)), ((), ()))


def once(a, b, dims=ROWS_COLS):
    return lax.dot_general(a.astype(BF16), b.astype(BF16), dims, preferred_element_type=F32)


def split(a):
    high = a.astype(BF16)
    return high, (a - high.astype(F32)).astype(BF16)


def thrice(a, b, dims=ROWS_COLS):
    a_high, a_low = split(a)
    b_high, b_low = split(b)
    dot = functools.partial(lax.dot_general, dimension_numbers=dims, preferred_element_type=F32)
    return dot(a_high, b_high) + (dot(a_high, b_low) + dot(a_low, b_high))


def iota(shape, dim):
    return lax.broadcasted_iota(jnp.int32, shape, dim)


def head_sum(array, first):
    low = jnp.sum(jnp.where(first, array, 0.0), -1, keepdims=True)
    high = jnp.sum(jnp.where(first, 0.0, array), -1, keepdims=True)
    return jnp.where(first, low, high)


def mixer_kernel(
    devices,
    rec_ref,
    key_ref,
    val_ref,
    rate_ref,
    learn_ref,
    scale_ref,
    shift_ref,
    reward_ref,
    center_ref,
    mixed_ref,
    enc_ref,
    local_s,
    probe_s,
    trans_s,
    own_s,
    arrive_s,
    leave_s,
    send_sem,
    recv_sem,
):
    me = lax.axis_index("ctx")
    tokens, width = rec_ref.shape
    chunk_lanes = PAIRS * LANES
    chunks = width // chunk_lanes

    barrier = pltpu.get_barrier_semaphore()
    for other in (lax.rem(me + 1, devices), lax.rem(me + devices - 1, devices)):
        pl.semaphore_signal(
            barrier, inc=1, device_id={"ctx": other}, device_id_type=pl.DeviceIdType.MESH
        )
    pl.semaphore_wait(barrier, 2)

    def lanes_of(chunk, pair):
        return pl.ds(pl.multiple_of(chunk * chunk_lanes + pair * LANES, LANES), LANES)

    def onward(chunk):
        return pltpu.make_async_remote_copy(
            src_ref=leave_s.at[chunk],
            dst_ref=arrive_s.at[chunk],
            send_sem=send_sem.at[chunk],
            recv_sem=recv_sem.at[chunk],
            device_id={"ctx": me + 1},
            device_id_type=pl.DeviceIdType.MESH,
        )

    def local(chunk):
        first = iota((tokens, LANES), 1) < ATTN_GROUP_DIM
        row = iota((tokens, tokens), 0)
        col = iota((tokens, tokens), 1)
        strict = row > col
        inclusive = row >= col
        same_head = (iota((LANES, LANES), 0) < ATTN_GROUP_DIM) == (
            iota((LANES, LANES), 1) < ATTN_GROUP_DIM
        )
        diagonal = iota((LANES, LANES), 0) == iota((LANES, LANES), 1)
        lower = inclusive.astype(F32).astype(BF16)
        identity = (row == col).astype(F32)

        todo = []
        for pair in range(PAIRS):
            at = lanes_of(chunk, pair)
            rec = rec_ref[:, at].astype(F32)
            key = key_ref[:, at].astype(F32)
            val = val_ref[:, at].astype(F32)
            rate = rate_ref[:, at].astype(F32)
            learn = learn_ref[:, at].astype(F32)
            total = lax.dot_general(
                lower, rate_ref[:, at], ROWS_COLS, preferred_element_type=F32
            )
            removal = key * lax.rsqrt(head_sum(key * key, first) + ATTN_GROUP_DIM * 1e-05)
            undo = jnp.exp(total)
            fade_to_end = jnp.exp(total - total[tokens - 1 :, :])
            left_a = -removal * jnp.exp(rate - total)
            left_r = rec * jnp.exp(-total)
            erase = removal * learn
            right = jnp.concatenate([erase * undo, key * undo], 0)
            ends = jnp.concatenate([erase * fade_to_end, key * fade_to_end], 0)
            fade = jnp.exp(-total[tokens - 1 :, :])
            sides = []
            for head in range(2):
                mine = first if head == 0 else jnp.logical_not(first)
                left = jnp.concatenate(
                    [jnp.where(mine, left_a, 0.0), jnp.where(mine, left_r, 0.0)], 0
                )
                gram = once(left, right, COLS_COLS)
                mix_ab = jnp.where(strict, gram[:tokens, :tokens], 0.0)
                mix_ak = jnp.where(strict, gram[:tokens, tokens:], 0.0)
                mix_rb = jnp.where(inclusive, gram[tokens:, :tokens], 0.0)
                mix_rk = jnp.where(inclusive, gram[tokens:, tokens:], 0.0)
                own_val = jnp.where(mine, val, 0.0)
                target = jnp.concatenate(
                    [once(mix_ak, own_val), jnp.where(mine, left_a, 0.0)], 1
                )
                sides.append((mix_ab, mix_rb, mix_rk, own_val, target))
            todo.append((at, left_r, val, ends, fade, sides))

        inverse = []
        for work in todo:
            for side in work[5]:
                pick = (row // 2 == col // 2)
                inverse.append(identity + jnp.where(pick, side[0], 0.0))
        size = 2
        while size < tokens:
            pick = (row // (2 * size) == col // (2 * size)) & (row // size != col // size)
            step = []
            index = 0
            for work in todo:
                for side in work[5]:
                    step.append(MM(inverse[index], jnp.where(pick, side[0], 0.0)))
                    index += 1
            inverse = [now + MM(part, now) for now, part in zip(inverse, step)]
            size *= 2

        for pair, (at, left_r, val, ends, fade, sides) in enumerate(todo):
            reads = [MM(inverse[2 * pair + head], sides[head][4]) for head in range(2)]
            both = reads[0] + reads[1]
            outs = once(
                jnp.concatenate([sides[0][1], sides[1][1]], 1), jnp.concatenate(reads, 0)
            )
            straight = once(
                jnp.concatenate([sides[0][2], sides[1][2]], 1),
                jnp.concatenate([sides[0][3], sides[1][3]], 0),
            )
            local_s[:, at] = outs[:, :LANES] + straight
            probe_s[:, at] = outs[:, LANES:] + left_r
            carry = once(both[:, LANES:], ends[:tokens], ROWS_ROWS)
            spot = chunk * PAIRS + pair
            trans_s[spot] = jnp.where(same_head, carry, 0.0) + jnp.where(diagonal, fade, 0.0)
            made = once(jnp.concatenate([both[:, :LANES], val], 0), ends, ROWS_ROWS)
            made = jnp.where(same_head, made, 0.0)
            own_s[spot] = made[:ATTN_GROUP_DIM] + made[ATTN_GROUP_DIM:]

    def finish(chunk):
        first = iota((tokens, LANES), 1) < ATTN_GROUP_DIM
        same_head = (iota((LANES, LANES), 0) < ATTN_GROUP_DIM) == (
            iota((LANES, LANES), 1) < ATTN_GROUP_DIM
        )
        for pair in range(PAIRS):
            at = lanes_of(chunk, pair)
            prior = arrive_s[chunk, pair]
            prior = jnp.where(same_head, jnp.concatenate([prior, prior], 0), 0.0)
            wkv = local_s[:, at] + once(probe_s[:, at], prior, COLS_COLS)
            center = wkv - head_sum(wkv, first) * (1.0 / ATTN_GROUP_DIM)
            spread = head_sum(center * center, first) * (1.0 / ATTN_GROUP_DIM)
            lines = center * lax.rsqrt(spread + 1e-05) * scale_ref[:, at] + shift_ref[:, at]
            bonus = head_sum(
                rec_ref[:, at].astype(F32) * key_ref[:, at].astype(F32) * reward_ref[:, at], first
            ) * val_ref[:, at].astype(F32)
            mixed = (lines + bonus).astype(BF16)
            mixed_ref[:, at] = mixed
            enc_ref[:, at] = (mixed.astype(F32) - center_ref[:, at]).astype(BF16)

    def chain(chunk):
        @pl.when(me == 0)
        def _():
            arrive_s[chunk] = jnp.zeros(arrive_s.shape[1:], F32)

        @pl.when(me > 0)
        def _():
            onward(chunk).wait_recv()

        @pl.when(me < devices - 1)
        def _():
            for pair in range(PAIRS):
                spot = chunk * PAIRS + pair
                leave_s[chunk, pair] = (
                    thrice(arrive_s[chunk, pair], trans_s[spot]) + own_s[spot]
                )
            onward(chunk).start()

        finish(chunk)

    def step(index, _):
        @pl.when(index < chunks)
        def _():
            local(index)

        late = index - me

        @pl.when((late >= 0) & (late < chunks))
        def _():
            chain(late)

        return 0

    lax.fori_loop(0, chunks + devices - 1, step, 0)

    @pl.when(me < devices - 1)
    def _():
        def drain(chunk, _):
            onward(chunk).wait_send()
            return 0

        lax.fori_loop(0, chunks, drain, 0)


MM = thrice


def mixer(devices, rec, key, val, rate, learn, scale, shift, reward, center):
    tokens, width = rec.shape
    chunks = width // (PAIRS * LANES)
    pairs = width // LANES
    shape = jax.ShapeDtypeStruct((tokens, width), BF16)
    vmem = pl.BlockSpec(memory_space=pltpu.VMEM)
    return pl.pallas_call(
        functools.partial(mixer_kernel, devices),
        out_shape=(shape, shape),
        in_specs=[vmem] * 9,
        out_specs=(vmem, vmem),
        scratch_shapes=[
            pltpu.VMEM((tokens, width), F32),
            pltpu.VMEM((tokens, width), F32),
            pltpu.VMEM((pairs, LANES, LANES), F32),
            pltpu.VMEM((pairs, ATTN_GROUP_DIM, LANES), F32),
            pltpu.VMEM((chunks, PAIRS, ATTN_GROUP_DIM, LANES), F32),
            pltpu.VMEM((chunks, PAIRS, ATTN_GROUP_DIM, LANES), F32),
            pltpu.SemaphoreType.DMA((chunks,)),
            pltpu.SemaphoreType.DMA((chunks,)),
        ],
        compiler_params=pltpu.CompilerParams(
            collective_id=0, has_side_effects=True, vmem_limit_bytes=40 * 1024 * 1024
        ),
        name="mixer",
    )(rec, key, val, rate, learn, scale[None], shift[None], reward[None], center[None])


def activate(preacts, mask_vals, index_vals, value_vals):
    senders, items, block_count = mask_vals.shape
    codes = jnp.maximum(preacts, 0.0).reshape(senders, items, TILE, block_count, BLK)
    within = lax.broadcasted_iota(jnp.int32, (block_count, BLK), 1)
    hit = within == index_vals[:, None]
    codes = jnp.where(hit, value_vals[:, None], codes)
    codes = codes * mask_vals.astype(jnp.float32)[:, :, None, :, None]
    return codes.reshape(senders * items * TILE, block_count * BLK).astype(jnp.bfloat16)


def body(
    gating_vectors,
    lookup_vectors,
    payload_vectors,
    forgetting_exponent,
    inline_adapt_factor,
    group_layer_scaling,
    group_layer_offset,
    present_reward_factor,
    shared_dictionary_matrix,
    sparse_code_offset,
    reconstruct_offset,
    panel_holder_choice,
    holder_group_enabled,
    fixed_feature_slot,
    fixed_feature_amount,
):
    tok_rows = gating_vectors.shape[0]
    feat_local = gating_vectors.shape[1]
    standardized_mixer_result, enc_in = mixer(
        lax.axis_size("ctx"),
        gating_vectors,
        lookup_vectors,
        payload_vectors,
        forgetting_exponent,
        inline_adapt_factor,
        group_layer_scaling,
        group_layer_offset,
        present_reward_factor,
        reconstruct_offset,
    )
    ctx_count = lax.axis_size("ctx")
    tile_count = tok_rows // TILE
    slot_count = panel_holder_choice.shape[1]
    blocks_own = holder_group_enabled.shape[2]
    capacity = max(2, 2 * tok_rows * slot_count // (TILE * ctx_count))
    pair_count = tile_count * slot_count
    owner_flat = panel_holder_choice.reshape(pair_count)
    earlier = (owner_flat[:, None] == owner_flat[None, :]) & (
        iota((pair_count, pair_count), 1) < iota((pair_count, pair_count), 0)
    )
    ranks = jnp.sum(earlier.astype(jnp.int32), axis=1)
    slot_ids = owner_flat * capacity + ranks
    dispatch = (
        slot_ids[None, :] == lax.broadcasted_iota(jnp.int32, (ctx_count * capacity, 1), 0)
    ).astype(jnp.float32)
    tile_pick = (
        lax.broadcasted_iota(jnp.int32, (tile_count, pair_count), 1) // slot_count
        == lax.broadcasted_iota(jnp.int32, (tile_count, pair_count), 0)
    ).astype(jnp.float32)
    slot_tile = jnp.dot(dispatch, tile_pick.T)
    send_rows = jnp.dot(
        slot_tile.astype(jnp.bfloat16),
        enc_in.reshape(tile_count, TILE * feat_local),
        preferred_element_type=jnp.float32,
    )
    send_rows = send_rows.astype(jnp.bfloat16).reshape(ctx_count, capacity, TILE, feat_local)
    send_mask = jnp.dot(
        dispatch, holder_group_enabled.reshape(pair_count, blocks_own).astype(jnp.float32)
    )
    send_mask = send_mask.astype(jnp.bfloat16).reshape(ctx_count, capacity, blocks_own)
    got_rows = lax.all_to_all(send_rows, "ctx", split_axis=0, concat_axis=0, tiled=True)
    got_mask = lax.all_to_all(send_mask, "ctx", split_axis=0, concat_axis=0, tiled=True)
    senders = got_rows.shape[0]
    items = got_rows.shape[1]
    flat_rows = got_rows.reshape(senders * items * TILE, feat_local)
    partial_pre = lax.dot_general(
        flat_rows,
        shared_dictionary_matrix,
        (((1,), (1,)), ((), ())),
        preferred_element_type=jnp.float32,
    )
    total_pre = lax.psum(partial_pre.astype(jnp.bfloat16), "width").astype(jnp.float32)
    codes = activate(
        total_pre + sparse_code_offset, got_mask, fixed_feature_slot, fixed_feature_amount
    )
    decoded = jnp.dot(codes, shared_dictionary_matrix, preferred_element_type=jnp.float32).astype(
        jnp.bfloat16
    )
    returned = decoded.reshape(senders, items, TILE, feat_local)
    received = lax.all_to_all(returned, "ctx", split_axis=0, concat_axis=0, tiled=True)
    summed = jnp.dot(
        slot_tile.T.astype(jnp.bfloat16),
        received.reshape(ctx_count * capacity, TILE * feat_local),
        preferred_element_type=jnp.float32,
    )
    steered = (summed.reshape(tok_rows, feat_local) + reconstruct_offset).astype(jnp.bfloat16)
    return (standardized_mixer_result, steered)


def solution(mesh):
    placed = (
        P(("groups", "ctx"), "width"),
        P(("groups", "ctx"), "width"),
        P(("groups", "ctx"), "width"),
        P(("groups", "ctx"), "width"),
        P(("groups", "ctx"), "width"),
        P("width"),
        P("width"),
        P("width"),
        P("ctx", "width"),
        P("ctx"),
        P("width"),
        P(("groups", "ctx"), None),
        P(("groups", "ctx"), None, None),
        P("ctx"),
        P("ctx"),
    )
    return jax.shard_map(
        body,
        mesh=mesh,
        in_specs=placed,
        out_specs=(P(("groups", "ctx"), "width"), P(("groups", "ctx"), "width")),
        check_vma=False,
    )
```

time: 525 us -> 234 us (0.45)
  waiting for transfers between devices: 200 us -> 66.1 us
  matrix products: 127 us -> 16.3 us
  Pallas kernels: 0 us -> 41.5 us
  local copies, waits for them, and re-layouts: 50.3 us -> 14.8 us
  starting transfers between devices: 41.5 us -> 9.78 us
  loops' own time: 16.2 us -> 0 us
  blocking collectives: 53.4 us -> 68.2 us
  other arithmetic: 15 us -> 1.15 us
    ppermute x7 -> x0, waiting for transfers between devices: 135 us -> none  [passed_along(): return lax.ppermute(block, axis, route)]
    dot_general x88 -> x0, matrix products: 107 us -> none  [the longest x7 15.6 us: forward(): jnp.einsum('hvj,hjk->hvk', incoming, transfer, precision=HIGHEST)]
    pallas_call x0 -> x1, Pallas kernels: none -> 41.5 us  [mixer(): pl.pallas_call(functools.partial(mixer_kernel, devices), out_shape=(shape...]
    ppermute x7 -> x0, starting transfers between devices: 32 us -> none  [passed_along(): return lax.ppermute(block, axis, route)]
    another operation x2 -> x0, loops' own time: 16.2 us -> none  [the longest x1 16.1 us: body(): lax.scan(block_step, start_state, (stacked(gating_vectors_all), stacked(l...]
    all_to_all x1, blocking collectives: 53.4 us -> 68.2 us  [body(): lax.all_to_all(send_rows, 'ctx', split_axis=0, concat_axis=0, tiled=True)]
    another operation x5 -> x0, local copies, waits for them, and re-layouts: 11.5 us -> none  [stacked(): return array.reshape(block_count, SUB, group_counting, ATTN_GROUP_DIM)]
    another operation x5 -> x0, other arithmetic: 7.85 us -> none  [the longest x4 7.79 us: block_step(): log_cum = -jnp.cumsum(rate_in, axis=0)]
  transfers between devices with their start and end apart: 10 -> 3, of which waited for: 10 -> 3; matrix products, arithmetic and copies ran while one was open for 0% -> 0% of each run, Pallas kernels for 0% -> 0%
where the time goes in v1:
time: 234 us; the launch traced here: 232 us
  blocking collectives  68.2 us (29%)
  waiting for transfers between devices  66.1 us (28%)
  Pallas kernels  41.5 us (18%)
  matrix products  16.3 us (7%)
  local copies, waits for them, and re-layouts  14.8 us (6%)
  between operations  14.2 us (6%)
  starting transfers between devices  9.78 us (4%)
    all_to_all x1, blocking collectives, body(): lax.all_to_all(send_rows, 'ctx', split_axis=0, concat_axis=0, tiled=True)  68.2 us
    all_to_all x1, waiting for transfers between devices, body(): lax.all_to_all(returned, 'ctx', split_axis=0, concat_axis=0, tiled=True)  47.8 us
    pallas_call x1, Pallas kernels, mixer(): pl.pallas_call(functools.partial(mixer_kernel, devices), out_shape=(shape...  41.5 us
    psum x1, waiting for transfers between devices, body(): lax.psum(partial_pre.astype(jnp.bfloat16), 'width').astype(jnp.float32)  13 us
    unnamed x35, local copies, waits for them, and re-layouts  11.2 us
    dot_general x1, matrix products, body(): jnp.dot(codes, shared_dictionary_matrix, preferred_element_type=jnp.float32)  9.06 us
    dot_general x1, matrix products, body(): lax.dot_general(flat_rows, shared_dictionary_matrix, (((1,), (1,)), ((),...  5.8 us
    all_to_all x1, starting transfers between devices, body(): lax.all_to_all(returned, 'ctx', split_axis=0, concat_axis=0, tiled=True)  5.58 us
  transfers between devices with their start and end apart: 3, of which 3 were waited for; matrix products, arithmetic and copies ran while one was open for 0% of the time, Pallas kernels for 0%

profile of v1, /device:TPU:1, one launch (start us, length us, event | category | flops | bytes accessed | tf_op | source)
XLA Modules:
  0.0 232.0 jit_solution(13577298202684539870)
XLA Ops:
  7.2 0.0 copy-start
  7.2 0.0 all-reduce.2.cloned.1.call-start
  7.2 0.8 copy.22
  8.0 0.1 reshape.52
  8.1 0.2 convert_reduce_fusion
  8.3 0.0 copy-start.1
  8.3 1.0 copy-done.1
  9.3 0.0 copy-start.2
  9.3 1.0 copy-done.2
  10.4 1.0 copy-done.3
  11.4 1.0 copy-done.4
  12.5 1.0 copy-done.5
  13.5 0.7 copy-done.6
  14.2 0.7 copy-done.8
  14.9 0.7 copy-done.9
  15.6 0.7 copy-done.10
  16.3 41.5 %mixer.1 = (bf16[128,2048]{1,0:T(8,128)(2,1)S(1)}, bf16[128,2048]{1,0:T(8,128)(2,1)S(1)}) custom-call(bf16[128,2048]{1,0:T(8,128)(2,1)S(1)} %copy-done.1, bf16[128,2048]{1,0:T(8,128)(2,1)S(1)} %copy-done.2, bf16[128,2048]{1,0:T(8,128)(2,1)S(1)} %copy-done.3, bf16[128,2048]{1,0:T(8,128)(2,1)S(1)} %copy-done.4, bf16[128,2048]{1,0:T(8,128)(2,1)S(1)} %copy-done.5, ...), custom_call_target="tpu_custom_call" | custom-call | tf_op jit(solution)/shard_map/mixer/pallas_call | solution.py:257
  57.8 0.2 reshape.53
  58.0 0.1 convolution_convert_fusion.4
  58.1 0.7 convolution_convert_fusion
  58.9 0.0 copy-start.13
  58.9 1.2 copy.23
  60.1 68.2 %all_to_all.15 = bf16[8,8,8,2048]{3,2,1,0:T(8,128)(2,1)S(1)} all-to-all(bf16[8,8,8,2048]{3,2,1,0:T(8,128)(2,1)S(1)} %copy.23), channel_id=1, replica_groups=mesh['groups'=2,'ctx'=8,'width'=2] {'ctx'}, dimensions={0} | all-to-all | bytes 4194304 | tf_op jit(solution)/shard_map/all_to_all | solution.py:350
  128.3 0.0 copy-done.13
  128.3 5.8 %convolution_convert_fusion.2 = bf16[512,2048]{1,0:T(8,128)(2,1)} fusion(bf16[512,2048]{1,0:T(8,128)(2,1)S(1)} %bitcast.33, bf16[2048,2048]{1,0:T(8,128)(2,1)S(1)} %copy-done.13), kind=kOutput, calls=%fused_computation.3 | convolution fusion | flops 4296015872 | bytes 12582912 | tf_op jit(solution)/shard_map/dot_general | solution.py:355
  134.1 0.0 all-reduce.2.cloned.1.call-update
  134.1 0.0 copy-done.11
  134.2 0.2 convolution_convert_fusion.3
  134.3 0.7 copy.24
  135.1 4.2 %all-to-all-start.1 = ((bf16[8,8,16]{2,1,0:T(8,128)(2,1)}), bf16[8,8,16]{2,1,0:T(8,128)(2,1)S(1)}, u32[]{:S(2)}, u32[]{:S(2)}) async-start(bf16[8,8,16]{2,1,0:T(8,128)(2,1)} %bitcast.9), calls=%async_computation.1 | async-start | bytes 32768 | tf_op jit(solution)/shard_map/all_to_all | solution.py:351
  139.2 0.0 copy-done
  139.2 0.1 broadcast_bitcast_fusion
  139.3 0.0 copy-done.12
  139.3 0.1 fusion.7
  139.4 5.3 %all-to-all-done.1 = bf16[8,8,16]{2,1,0:T(8,128)(2,1)S(1)} async-done(((bf16[8,8,16]{2,1,0:T(8,128)(2,1)}), bf16[8,8,16]{2,1,0:T(8,128)(2,1)S(1)}, u32[]{:S(2)}, u32[]{:S(2)}) %all-to-all-start.1) | async-done | bytes 2080 | tf_op jit(solution)/shard_map/all_to_all | solution.py:351
  144.6 13.0 %all-reduce.2.cloned.1.call-done = bf16[512,2048]{1,0:T(8,128)(2,1)} async-done(((bf16[512,2048]{1,0:T(8,128)(2,1)}), bf16[512,2048]{1,0:T(8,128)(2,1)}) %all-reduce.2.cloned.1.call-update) | async-done | bytes 2097168 | tf_op jit(solution)/shard_map/psum | solution.py:361
  157.7 1.1 mul.23
  158.8 0.0 copy-done.15
  158.8 0.4 copy-done.14
  159.2 9.1 %convolution_convert_fusion.1 = bf16[512,2048]{1,0:T(8,128)(2,1)} fusion(bf16[2048,2048]{1,0:T(8,128)(2,1)} %param.23, f32[512,2048]{1,0:T(8,128)S(1)} %bitcast.31, bf16[512,2048]{1,0:T(8,128)(2,1)S(1)} %copy-done.14, f32[2048]{0:T(1024)S(1)} %copy-done.15, f32[2048]{0:T(1024)S(1)} %broadcast_bitcast_fusion, pred[2048]{0:T(1024)(128)(4,1)S(1)} %fusion.7), kind=kOutput, calls=%fused_computation.2 | convolution fusion | flops 4302307328 | bytes 16795648 | tf_op jit(solution)/shard_map/dot_general | solution.py:365
  168.3 5.6 %all-to-all-start.2 = ((bf16[8,8,8,2048]{3,2,1,0:T(8,128)(2,1)}), bf16[8,8,8,2048]{3,2,1,0:T(8,128)(2,1)S(1)}, u32[]{:S(2)}, u32[]{:S(2)}) async-start(bf16[8,8,8,2048]{3,2,1,0:T(8,128)(2,1)} %bitcast.32), calls=%async_computation.2 | async-start | bytes 4194304 | tf_op jit(solution)/shard_map/all_to_all | solution.py:369
  173.9 47.8 %all-to-all-done.2 = bf16[8,8,8,2048]{3,2,1,0:T(8,128)(2,1)S(1)} async-done(((bf16[8,8,8,2048]{3,2,1,0:T(8,128)(2,1)}), bf16[8,8,8,2048]{3,2,1,0:T(8,128)(2,1)S(1)}, u32[]{:S(2)}, u32[]{:S(2)}) %all-to-all-start.2) | async-done | bytes 2097184 | tf_op jit(solution)/shard_map/all_to_all | solution.py:369
  221.7 1.2 copy.25
  222.9 0.4 fusion.12
  223.3 0.2 reshape.59
  223.5 0.0 copy-done.7
  223.5 0.9 add_convert_fusion
  224.4 0.8 copy.28
  (16 shorter events, 0.0 us)
Async XLA Ops:
  7.2 132.1 %copy-start = (f32[16]{0:T(128)S(1)}, f32[16]{0:T(128)}, u32[]{:S(2)}) copy-start(f32[16]{0:T(128)} %param.29) | copy-start | bytes 196
  7.2 150.5 %all-reduce.2.cloned.1.call-start = ((), (), s32[]{:S(2)}) async-start(), calls=%async_computation.3 | async-start | bytes 4194304 | tf_op jit(solution)/shard_map/psum | solution.py:361
  8.3 1.0 copy-start.1
  9.3 1.0 copy-start.2
  10.4 1.0 copy-start.3
  11.4 1.0 copy-start.4
  12.5 1.0 copy-start.5
  13.5 0.7 copy-start.6
  14.2 0.7 copy-start.8
  14.9 0.7 copy-start.9
  15.6 0.7 copy-start.10
  58.9 69.4 %copy-start.13 = (bf16[2048,2048]{1,0:T(8,128)(2,1)S(1)}, bf16[2048,2048]{1,0:T(8,128)(2,1)}, u32[]{:S(2)}) copy-start(bf16[2048,2048]{1,0:T(8,128)(2,1)} %param.23) | copy-start | bytes 25165828
  128.3 5.8 %copy-start.11 = (s32[16,2,16]{2,1,0:T(2,128)S(1)}, s32[16,2,16]{2,1,0:T(2,128)}, u32[]{:S(2)}) copy-start(s32[16,2,16]{2,1,0:T(2,128)} %param.27) | copy-start | bytes 6148
  128.3 11.0 %copy-start.12 = (s32[16]{0:T(128)S(1)}, s32[16]{0:T(128)}, u32[]{:S(2)}) copy-start(s32[16]{0:T(128)} %param.28) | copy-start | bytes 196
  134.1 24.7 %copy-start.15 = (f32[2048]{0:T(1024)S(1)}, f32[2048]{0:T(1024)}, u32[]{:S(2)}) copy-start(f32[2048]{0:T(1024)} %param.24) | copy-start | bytes 24580
  135.1 9.6 %all-to-all-start.1 = ((bf16[8,8,16]{2,1,0:T(8,128)(2,1)}), bf16[8,8,16]{2,1,0:T(8,128)(2,1)S(1)}, u32[]{:S(2)}, u32[]{:S(2)}) async-start(bf16[8,8,16]{2,1,0:T(8,128)(2,1)} %bitcast.9), calls=%async_computation.1 | async-start | bytes 32768 | tf_op jit(solution)/shard_map/all_to_all | solution.py:351
  157.7 1.6 copy-start.14
  168.3 53.4 %all-to-all-start.2 = ((bf16[8,8,8,2048]{3,2,1,0:T(8,128)(2,1)}), bf16[8,8,8,2048]{3,2,1,0:T(8,128)(2,1)S(1)}, u32[]{:S(2)}, u32[]{:S(2)}) async-start(bf16[8,8,8,2048]{3,2,1,0:T(8,128)(2,1)} %bitcast.32), calls=%async_computation.2 | async-start | bytes 4194304 | tf_op jit(solution)/shard_map/all_to_all | solution.py:369
  173.9 49.6 %copy-start.7 = (f32[2048]{0:T(1024)S(1)}, f32[2048]{0:T(1024)}, u32[]{:S(2)}) copy-start(f32[2048]{0:T(1024)} %param.25) | copy-start | bytes 24580
Sparse Core Ops, SparseCore 0:
  134.3 23.3 all-reduce.1

commit v2 on v1

--- a/solution.py
+++ b/solution.py
@@ -47,7 +47,7 @@
     return jnp.where(first, low, high)
 
 
-def mixer_kernel(
+def whole_kernel(
     devices,
     rec_ref,
     key_ref,
@@ -58,28 +58,122 @@
     shift_ref,
     reward_ref,
     center_ref,
+    spread_ref,
+    gather_ref,
+    tile_mask_ref,
+    bias_ref,
+    hit_ref,
+    forced_ref,
+    table_ref,
     mixed_ref,
-    enc_ref,
+    steered_ref,
     local_s,
     probe_s,
     trans_s,
     own_s,
     arrive_s,
     leave_s,
+    table_s,
+    stage_s,
+    got_s,
+    mask_s,
+    pre_s,
+    half_s,
+    peer_s,
+    codes_s,
+    part_s,
+    back_s,
     send_sem,
     recv_sem,
+    table_sem,
+    out_sem,
+    in_sem,
+    mask_out_sem,
+    mask_in_sem,
+    half_out_sem,
+    half_in_sem,
+    part_out_sem,
+    part_in_sem,
 ):
     me = lax.axis_index("ctx")
+    peer = 1 - lax.axis_index("width")
     tokens, width = rec_ref.shape
     chunk_lanes = PAIRS * LANES
     chunks = width // chunk_lanes
+    latents = bias_ref.shape[1]
+    rows = spread_ref.shape[0]
+    pair_rows = rows // devices
+    strips = latents // STRIP
+
+    table_copy = pltpu.make_async_copy(table_ref, table_s, table_sem)
+    table_copy.start()
 
     barrier = pltpu.get_barrier_semaphore()
-    for other in (lax.rem(me + 1, devices), lax.rem(me + devices - 1, devices)):
+
+    def greet(hop, _):
         pl.semaphore_signal(
-            barrier, inc=1, device_id={"ctx": other}, device_id_type=pl.DeviceIdType.MESH
-        )
-    pl.semaphore_wait(barrier, 2)
+            barrier,
+            inc=1,
+            device_id={"ctx": lax.rem(me + hop, devices)},
+            device_id_type=pl.DeviceIdType.MESH,
+        )
+        return 0
+
+    lax.fori_loop(1, devices, greet, 0)
+    pl.semaphore_signal(
+        barrier, inc=1, device_id={"width": peer}, device_id_type=pl.DeviceIdType.MESH
+    )
+    pl.semaphore_wait(barrier, devices)
+
+    def mask_copy(source, owner, sender):
+        return pltpu.make_async_remote_copy(
+            src_ref=tile_mask_ref.at[source],
+            dst_ref=mask_s.at[sender],
+            send_sem=mask_out_sem.at[owner],
+            recv_sem=mask_in_sem.at[sender],
+            device_id={"ctx": owner},
+            device_id_type=pl.DeviceIdType.MESH,
+        )
+
+    def row_copy(chunk, owner, sender):
+        return pltpu.make_async_remote_copy(
+            src_ref=stage_s.at[chunk, owner],
+            dst_ref=got_s.at[chunk, sender],
+            send_sem=out_sem.at[chunk, owner],
+            recv_sem=in_sem.at[chunk, sender],
+            device_id={"ctx": owner},
+            device_id_type=pl.DeviceIdType.MESH,
+        )
+
+    def part_copy(chunk, home, owner):
+        return pltpu.make_async_remote_copy(
+            src_ref=part_s.at[chunk, home],
+            dst_ref=back_s.at[chunk, owner],
+            send_sem=part_out_sem.at[chunk, home],
+            recv_sem=part_in_sem.at[chunk, owner],
+            device_id={"ctx": home},
+            device_id_type=pl.DeviceIdType.MESH,
+        )
+
+    def half_copy(strip):
+        return pltpu.make_async_remote_copy(
+            src_ref=half_s.at[strip],
+            dst_ref=peer_s.at[strip],
+            send_sem=half_out_sem.at[strip],
+            recv_sem=half_in_sem.at[strip],
+            device_id={"width": peer},
+            device_id_type=pl.DeviceIdType.MESH,
+        )
+
+    def others(visit):
+        def hop_to(hop, _):
+            visit(lax.rem(me + hop, devices))
+            return 0
+
+        lax.fori_loop(1, devices, hop_to, 0)
+
+    others(lambda other: mask_copy(other, other, me).start())
+    mask_s[me] = tile_mask_ref[me]
 
     def lanes_of(chunk, pair):
         return pl.ds(pl.multiple_of(chunk * chunk_lanes + pair * LANES, LANES), LANES)
@@ -199,7 +293,13 @@
             ) * val_ref[:, at].astype(F32)
             mixed = (lines + bonus).astype(BF16)
             mixed_ref[:, at] = mixed
-            enc_ref[:, at] = (mixed.astype(F32) - center_ref[:, at]).astype(BF16)
+            enc = (mixed.astype(F32) - center_ref[:, at]).astype(BF16)
+            placed = once(spread_ref[...], enc).astype(BF16)
+            stage_s[chunk, :, :, pair * LANES : (pair + 1) * LANES] = placed.reshape(
+                devices, pair_rows, LANES
+            )
+        others(lambda other: row_copy(chunk, other, me).start())
+        got_s[chunk, me] = stage_s[chunk, me]
 
     def chain(chunk):
         @pl.when(me == 0)
@@ -236,28 +336,120 @@
 
     lax.fori_loop(0, chunks + devices - 1, step, 0)
 
-    @pl.when(me < devices - 1)
-    def _():
-        def drain(chunk, _):
+    table_copy.wait()
+    others(lambda other: mask_copy(other, me, other).wait_recv())
+
+    def chunk_at(chunk):
+        return pl.ds(pl.multiple_of(chunk * chunk_lanes, chunk_lanes), chunk_lanes)
+
+    def strip_at(strip):
+        return pl.ds(pl.multiple_of(strip * STRIP, STRIP), STRIP)
+
+    def encoded(chunk, strip):
+        return lax.dot_general(
+            got_s[chunk].reshape(rows, chunk_lanes),
+            table_s[strip_at(strip), chunk_at(chunk)],
+            COLS_COLS,
+            preferred_element_type=F32,
+        )
+
+    def encode(chunk, _):
+        others(lambda other: row_copy(chunk, me, other).wait_recv())
+
+        def one(strip, _):
+            @pl.when(chunk == 0)
+            def _():
+                pre_s[strip] = encoded(chunk, strip)
+
+            @pl.when(chunk > 0)
+            def _():
+                pre_s[strip] += encoded(chunk, strip)
+
+            @pl.when(chunk == chunks - 1)
+            def _():
+                half_s[strip] = pre_s[strip].astype(BF16)
+                half_copy(strip).start()
+
+            return 0
+
+        lax.fori_loop(0, strips, one, 0)
+        return 0
+
+    lax.fori_loop(0, chunks, encode, 0)
+
+    for strip in range(strips):
+        half_copy(strip).wait_recv()
+        for block in range(STRIP // BLK):
+            inside = slice(block * BLK, (block + 1) * BLK)
+            at = slice(strip * STRIP + block * BLK, strip * STRIP + (block + 1) * BLK)
+            pre = pre_s[strip, :, inside] + peer_s[strip, :, inside].astype(F32)
+            code = jnp.maximum(pre + bias_ref[:, at], 0.0)
+            code = jnp.where(hit_ref[:, at] > 0.0, forced_ref[:, at], code)
+            index = strip * (STRIP // BLK) + block
+            active = mask_s[:, :, index : index + 1].reshape(rows, 1).astype(F32)
+            codes_s[:, at] = (code * active).astype(BF16)
+
+    def decode(chunk, _):
+        part = lax.dot_general(
+            codes_s[...], table_s[:, chunk_at(chunk)], ROWS_COLS, preferred_element_type=F32
+        )
+        part_s[chunk] = part.astype(BF16).reshape(devices, pair_rows, chunk_lanes)
+        others(lambda other: part_copy(chunk, other, me).start())
+        back_s[chunk, me] = part_s[chunk, me]
+        return 0
+
+    lax.fori_loop(0, chunks, decode, 0)
+
+    def combine(chunk, _):
+        others(lambda other: part_copy(chunk, me, other).wait_recv())
+        at = chunk_at(chunk)
+        total = lax.dot_general(
+            gather_ref[...],
+            back_s[chunk].reshape(rows, chunk_lanes),
+            ROWS_COLS,
+            preferred_element_type=F32,
+        )
+        steered_ref[:, at] = (total + center_ref[:, at]).astype(BF16)
+        return 0
+
+    lax.fori_loop(0, chunks, combine, 0)
+
+    def drain(chunk, _):
+        @pl.when(me < devices - 1)
+        def _():
             onward(chunk).wait_send()
-            return 0
-
-        lax.fori_loop(0, chunks, drain, 0)
+
+        others(lambda other: row_copy(chunk, other, me).wait_send())
+        others(lambda other: part_copy(chunk, other, me).wait_send())
+        return 0
+
+    lax.fori_loop(0, chunks, drain, 0)
+    others(lambda other: mask_copy(other, other, me).wait_send())
+    for strip in range(strips):
+        half_copy(strip).wait_send()
 
 
 MM = thrice
-
-
-def mixer(devices, rec, key, val, rate, learn, scale, shift, reward, center):
+STRIP = 512
+
+
+def whole(devices, rec, key, val, rate, learn, lines, spread, gather, tile_mask, latent_lines, table):
     tokens, width = rec.shape
     chunks = width // (PAIRS * LANES)
     pairs = width // LANES
+    latents = table.shape[0]
+    rows = spread.shape[0]
+    pair_rows = rows // devices
+    strips = latents // STRIP
     shape = jax.ShapeDtypeStruct((tokens, width), BF16)
     vmem = pl.BlockSpec(memory_space=pltpu.VMEM)
+    blocks = pltpu.VMEM((chunks, devices, pair_rows, PAIRS * LANES), BF16)
+    strip_rows = pltpu.VMEM((strips, rows, STRIP), BF16)
+    dma = pltpu.SemaphoreType.DMA
     return pl.pallas_call(
-        functools.partial(mixer_kernel, devices),
+        functools.partial(whole_kernel, devices),
         out_shape=(shape, shape),
-        in_specs=[vmem] * 9,
+        in_specs=[vmem] * 15 + [pl.BlockSpec(memory_space=pl.ANY)],
         out_specs=(vmem, vmem),
         scratch_shapes=[
             pltpu.VMEM((tokens, width), F32),
@@ -266,24 +458,33 @@
             pltpu.VMEM((pairs, ATTN_GROUP_DIM, LANES), F32),
             pltpu.VMEM((chunks, PAIRS, ATTN_GROUP_DIM, LANES), F32),
             pltpu.VMEM((chunks, PAIRS, ATTN_GROUP_DIM, LANES), F32),
-            pltpu.SemaphoreType.DMA((chunks,)),
-            pltpu.SemaphoreType.DMA((chunks,)),
+            pltpu.VMEM((latents, width), BF16),
+            blocks,
+            blocks,
+            pltpu.VMEM((devices, pair_rows, LANES), BF16),
+            pltpu.VMEM((strips, rows, STRIP), F32),
+            strip_rows,
+            strip_rows,
+            pltpu.VMEM((rows, latents), BF16),
+            blocks,
+            blocks,
+            dma((chunks,)),
+            dma((chunks,)),
+            dma,
+            dma((chunks, devices)),
+            dma((chunks, devices)),
+            dma((devices,)),
+            dma((devices,)),
+            dma((strips,)),
+            dma((strips,)),
+            dma((chunks, devices)),
+            dma((chunks, devices)),
         ],
         compiler_params=pltpu.CompilerParams(
-            collective_id=0, has_side_effects=True, vmem_limit_bytes=40 * 1024 * 1024
+            collective_id=0, has_side_effects=True, vmem_limit_bytes=52 * 1024 * 1024
         ),
-        name="mixer",
-    )(rec, key, val, rate, learn, scale[None], shift[None], reward[None], center[None])
-
-
-def activate(preacts, mask_vals, index_vals, value_vals):
-    senders, items, block_count = mask_vals.shape
-    codes = jnp.maximum(preacts, 0.0).reshape(senders, items, TILE, block_count, BLK)
-    within = lax.broadcasted_iota(jnp.int32, (block_count, BLK), 1)
-    hit = within == index_vals[:, None]
-    codes = jnp.where(hit, value_vals[:, None], codes)
-    codes = codes * mask_vals.astype(jnp.float32)[:, :, None, :, None]
-    return codes.reshape(senders * items * TILE, block_count * BLK).astype(jnp.bfloat16)
+        name="whole",
+    )(rec, key, val, rate, learn, *lines, spread, gather, tile_mask, *latent_lines, table)
 
 
 def body(
@@ -304,19 +505,6 @@
     fixed_feature_amount,
 ):
     tok_rows = gating_vectors.shape[0]
-    feat_local = gating_vectors.shape[1]
-    standardized_mixer_result, enc_in = mixer(
-        lax.axis_size("ctx"),
-        gating_vectors,
-        lookup_vectors,
-        payload_vectors,
-        forgetting_exponent,
-        inline_adapt_factor,
-        group_layer_scaling,
-        group_layer_offset,
-        present_reward_factor,
-        reconstruct_offset,
-    )
     ctx_count = lax.axis_size("ctx")
     tile_count = tok_rows // TILE
     slot_count = panel_holder_choice.shape[1]
@@ -337,43 +525,37 @@
         == lax.broadcasted_iota(jnp.int32, (tile_count, pair_count), 0)
     ).astype(jnp.float32)
     slot_tile = jnp.dot(dispatch, tile_pick.T)
-    send_rows = jnp.dot(
-        slot_tile.astype(jnp.bfloat16),
-        enc_in.reshape(tile_count, TILE * feat_local),
-        preferred_element_type=jnp.float32,
-    )
-    send_rows = send_rows.astype(jnp.bfloat16).reshape(ctx_count, capacity, TILE, feat_local)
-    send_mask = jnp.dot(
+    each = jnp.eye(TILE, dtype=jnp.float32)
+    rows = ctx_count * capacity * TILE
+    spread = (
+        (slot_tile[:, None, :, None] * each[None, :, None, :])
+        .reshape(rows, tok_rows)
+        .astype(jnp.bfloat16)
+    )
+    tile_mask = jnp.dot(
         dispatch, holder_group_enabled.reshape(pair_count, blocks_own).astype(jnp.float32)
     )
-    send_mask = send_mask.astype(jnp.bfloat16).reshape(ctx_count, capacity, blocks_own)
-    got_rows = lax.all_to_all(send_rows, "ctx", split_axis=0, concat_axis=0, tiled=True)
-    got_mask = lax.all_to_all(send_mask, "ctx", split_axis=0, concat_axis=0, tiled=True)
-    senders = got_rows.shape[0]
-    items = got_rows.shape[1]
-    flat_rows = got_rows.reshape(senders * items * TILE, feat_local)
-    partial_pre = lax.dot_general(
-        flat_rows,
+    tile_mask = jnp.pad(tile_mask, ((0, 0), (0, LANES - blocks_own)))
+    tile_mask = jnp.broadcast_to(tile_mask[:, None, :], (ctx_count * capacity, TILE, LANES))
+    tile_mask = tile_mask.astype(jnp.bfloat16).reshape(ctx_count, capacity * TILE, LANES)
+    within = lax.broadcasted_iota(jnp.int32, (blocks_own, BLK), 1)
+    hit = (within == fixed_feature_slot[:, None]).astype(jnp.float32).reshape(1, -1)
+    forced = jnp.broadcast_to(fixed_feature_amount[:, None], (blocks_own, BLK)).reshape(1, -1)
+    lines = (group_layer_scaling, group_layer_offset, present_reward_factor, reconstruct_offset)
+    return whole(
+        ctx_count,
+        gating_vectors,
+        lookup_vectors,
+        payload_vectors,
+        forgetting_exponent,
+        inline_adapt_factor,
+        tuple(line[None] for line in lines),
+        spread,
+        spread.T,
+        tile_mask,
+        (sparse_code_offset[None], hit, forced),
         shared_dictionary_matrix,
-        (((1,), (1,)), ((), ())),
-        preferred_element_type=jnp.float32,
-    )
-    total_pre = lax.psum(partial_pre.astype(jnp.bfloat16), "width").astype(jnp.float32)
-    codes = activate(
-        total_pre + sparse_code_offset, got_mask, fixed_feature_slot, fixed_feature_amount
-    )
-    decoded = jnp.dot(codes, shared_dictionary_matrix, preferred_element_type=jnp.float32).astype(
-        jnp.bfloat16
-    )
-    returned = decoded.reshape(senders, items, TILE, feat_local)
-    received = lax.all_to_all(returned, "ctx", split_axis=0, concat_axis=0, tiled=True)
-    summed = jnp.dot(
-        slot_tile.T.astype(jnp.bfloat16),
-        received.reshape(ctx_count * capacity, TILE * feat_local),
-        preferred_element_type=jnp.float32,
-    )
-    steered = (summed.reshape(tok_rows, feat_local) + reconstruct_offset).astype(jnp.bfloat16)
-    return (standardized_mixer_result, steered)
+    )
 
 
 def solution(mesh):

time: 234 us -> 155 us (0.66)
  Pallas kernels: 41.5 us -> 148 us
  blocking collectives: 68.2 us -> 0 us
  waiting for transfers between devices: 66.1 us -> 0 us
  matrix products: 16.3 us -> 0.31 us
  between operations: 14.2 us -> 0.84 us
  local copies, waits for them, and re-layouts: 14.8 us -> 5.01 us
  starting transfers between devices: 9.78 us -> 0 us
    pallas_call x1, Pallas kernels: 41.5 us -> 148 us  [whole(): pl.pallas_call(functools.partial(whole_kernel, devices), out_shape=(shape...]
    all_to_all x1 -> x0, blocking collectives: 68.2 us -> none  [body(): lax.all_to_all(send_rows, 'ctx', split_axis=0, concat_axis=0, tiled=True)]
    all_to_all x2 -> x0, waiting for transfers between devices: 53.1 us -> none  [the longest x1 47.8 us: body(): lax.all_to_all(returned, 'ctx', split_axis=0, concat_axis=0, tiled=True)]
    dot_general x4 -> x0, matrix products: 16 us -> none  [the longest x1 9.06 us: body(): jnp.dot(codes, shared_dictionary_matrix, preferred_element_type=jnp.float32)]
    psum x1 -> x0, waiting for transfers between devices: 13 us -> none  [body(): lax.psum(partial_pre.astype(jnp.bfloat16), 'width').astype(jnp.float32)]
    all_to_all x2 -> x0, starting transfers between devices: 9.74 us -> none  [the longest x1 5.58 us: body(): lax.all_to_all(returned, 'ctx', split_axis=0, concat_axis=0, tiled=True)]
    unnamed x35 -> x22, local copies, waits for them, and re-layouts: 11.2 us -> 2.54 us
  transfers between devices with their start and end apart: 3 -> 0, of which waited for: 3 -> 0; matrix products, arithmetic and copies ran while one was open for 0% -> 0% of each run, Pallas kernels for 0% -> 0%
where the time goes in v2:
time: 155 us
  Pallas kernels  148 us (95%)
  local copies, waits for them, and re-layouts  5.01 us (3%)
    pallas_call x1, Pallas kernels, whole(): pl.pallas_call(functools.partial(whole_kernel, devices), out_shape=(shape...  148 us

profile of v2, /device:TPU:1, one launch (start us, length us, event | category | flops | bytes accessed | tf_op | source)
XLA Modules:
  0.0 154.8 jit_solution(18088126057262898201)
XLA Ops:
  0.6 0.0 copy-start.6
  0.6 0.0 copy-start.7
  0.7 0.0 copy-start.8
  0.7 0.0 copy-start.1
  0.7 0.0 copy-start.2
  0.7 0.0 copy-start.3
  0.7 0.0 copy-start.4
  0.7 0.0 copy-start.5
  0.7 0.0 copy-start
  0.7 0.8 copy.24
  1.5 0.1 reshape.70
  1.6 0.2 convert_reduce_fusion
  1.8 0.1 fusion
  2.0 0.4 multiply_convert_fusion
  2.4 2.2 %convert_element_type.43.spread_ref = bf16[512,128]{1,0:T(8,128)(2,1)S(1)} reshape(bf16[64,8,16,8]{3,2,1,0:T(8,128)(2,1)S(1)} %multiply_convert_fusion) | data formatting | bytes 262144 | tf_op jit(solution)/shard_map/convert_element_type | solution.py:533
  4.6 0.1 copy.26
  4.7 0.0 copy-done.6
  4.7 0.2 convolution_convert_fusion
  4.9 0.1 copy.29
  5.0 0.0 copy-done.7
  5.1 0.1 fusion.4
  5.1 0.0 copy-done.8
  5.1 0.1 broadcast_in_dim.37
  5.2 0.0 copy-done.1
  5.2 0.0 copy-done.2
  5.2 0.0 copy-done.3
  5.2 0.0 copy-done.4
  5.2 0.0 copy-done.5
  5.2 0.0 copy-done
  5.2 147.9 %whole.1 = (bf16[128,2048]{1,0:T(8,128)(2,1)S(1)}, bf16[128,2048]{1,0:T(8,128)(2,1)S(1)}) custom-call(bf16[128,2048]{1,0:T(8,128)(2,1)S(1)} %copy-done, bf16[128,2048]{1,0:T(8,128)(2,1)} %key_ref.1, bf16[128,2048]{1,0:T(8,128)(2,1)} %val_ref.1, bf16[128,2048]{1,0:T(8,128)(2,1)} %rate_ref.1, bf16[128,2048]{1,0:T(8,128)(2,1)} %learn_ref.1, ...), custom_call_target="tpu_custom_call" | custom-call | tf_op jit(solution)/shard_map/whole/pallas_call | solution.py:449
  153.2 0.8 copy.32
  154.0 0.8 copy.33
  (7 shorter events, 0.1 us)
Async XLA Ops:
  0.6 4.1 %copy-start.6 = (s32[16,2,16]{2,1,0:T(2,128)S(1)}, s32[16,2,16]{2,1,0:T(2,128)}, u32[]{:S(2)}) copy-start(s32[16,2,16]{2,1,0:T(2,128)} %param.27) | copy-start | bytes 6148
  0.6 4.4 %copy-start.7 = (s32[16]{0:T(128)S(1)}, s32[16]{0:T(128)}, u32[]{:S(2)}) copy-start(s32[16]{0:T(128)} %param.28) | copy-start | bytes 196
  0.7 4.5 %copy-start.8 = (f32[16]{0:T(128)S(1)}, f32[16]{0:T(128)}, u32[]{:S(2)}) copy-start(f32[16]{0:T(128)} %param.29) | copy-start | bytes 196
  0.7 4.5 %copy-start.1 = (f32[2048]{0:T(1024)S(1)}, f32[2048]{0:T(1024)}, u32[]{:S(2)}) copy-start(f32[2048]{0:T(1024)} %param.20) | copy-start | bytes 24580
  0.7 4.5 %copy-start.2 = (f32[2048]{0:T(1024)S(1)}, f32[2048]{0:T(1024)}, u32[]{:S(2)}) copy-start(f32[2048]{0:T(1024)} %param.21) | copy-start | bytes 24580
  0.7 4.5 %copy-start.3 = (f32[2048]{0:T(1024)S(1)}, f32[2048]{0:T(1024)}, u32[]{:S(2)}) copy-start(f32[2048]{0:T(1024)} %param.22) | copy-start | bytes 24580
  0.7 4.5 %copy-start.4 = (f32[2048]{0:T(1024)S(1)}, f32[2048]{0:T(1024)}, u32[]{:S(2)}) copy-start(f32[2048]{0:T(1024)} %param.25) | copy-start | bytes 24580
  0.7 4.5 %copy-start.5 = (f32[2048]{0:T(1024)S(1)}, f32[2048]{0:T(1024)}, u32[]{:S(2)}) copy-start(f32[2048]{0:T(1024)} %param.24) | copy-start | bytes 24580
  0.7 4.5 %copy-start = (bf16[128,2048]{1,0:T(8,128)(2,1)S(1)}, bf16[128,2048]{1,0:T(8,128)(2,1)}, u32[]{:S(2)}) copy-start(bf16[128,2048]{1,0:T(8,128)(2,1)} %rec_ref.1) | copy-start | bytes 1572868

commit v3 on v2

--- a/solution.py
+++ b/solution.py
@@ -30,11 +30,15 @@
     return high, (a - high.astype(F32)).astype(BF16)
 
 
-def thrice(a, b, dims=ROWS_COLS):
+def fine(a, b):
     a_high, a_low = split(a)
     b_high, b_low = split(b)
-    dot = functools.partial(lax.dot_general, dimension_numbers=dims, preferred_element_type=F32)
-    return dot(a_high, b_high) + (dot(a_high, b_low) + dot(a_low, b_high))
+    left = jnp.concatenate([a_high, a_low], 1)
+    if b.shape[1] == LANES:
+        right = jnp.concatenate([b_high, b_low], 1)
+        both = once(left, jnp.concatenate([right, right], 0))
+        return both[:, :LANES] + both[:, LANES:]
+    return once(left, jnp.concatenate([b_high, b_high], 0)) + once(a_high, b_low)
 
 
 def iota(shape, dim):
@@ -58,8 +62,7 @@
     shift_ref,
     reward_ref,
     center_ref,
-    spread_ref,
-    gather_ref,
+    placing_ref,
     tile_mask_ref,
     bias_ref,
     hit_ref,
@@ -73,6 +76,8 @@
     own_s,
     arrive_s,
     leave_s,
+    spread_s,
+    gather_s,
     table_s,
     stage_s,
     got_s,
@@ -100,8 +105,8 @@
     tokens, width = rec_ref.shape
     chunk_lanes = PAIRS * LANES
     chunks = width // chunk_lanes
-    latents = bias_ref.shape[1]
-    rows = spread_ref.shape[0]
+    latents = bias_ref.shape[0] * BLK
+    rows = placing_ref.shape[1]
     pair_rows = rows // devices
     strips = latents // STRIP
 
@@ -174,6 +179,9 @@
 
     others(lambda other: mask_copy(other, other, me).start())
     mask_s[me] = tile_mask_ref[me]
+    gather = (placing_ref[...] == iota((tokens, rows), 0)).astype(F32)
+    gather_s[...] = gather.astype(BF16)
+    spread_s[...] = gather.T.astype(BF16)
 
     def lanes_of(chunk, pair):
         return pl.ds(pl.multiple_of(chunk * chunk_lanes + pair * LANES, LANES), LANES)
@@ -221,13 +229,18 @@
             right = jnp.concatenate([erase * undo, key * undo], 0)
             ends = jnp.concatenate([erase * fade_to_end, key * fade_to_end], 0)
             fade = jnp.exp(-total[tokens - 1 :, :])
+            right_high, right_low = split(right)
+            right_twice = jnp.concatenate([right_high, right_high], 1)
             sides = []
             for head in range(2):
                 mine = first if head == 0 else jnp.logical_not(first)
                 left = jnp.concatenate(
                     [jnp.where(mine, left_a, 0.0), jnp.where(mine, left_r, 0.0)], 0
                 )
-                gram = once(left, right, COLS_COLS)
+                left_high, left_low = split(left)
+                gram = once(
+                    jnp.concatenate([left_high, left_low], 1), right_twice, COLS_COLS
+                ) + once(left_high, right_low, COLS_COLS)
                 mix_ab = jnp.where(strict, gram[:tokens, :tokens], 0.0)
                 mix_ak = jnp.where(strict, gram[:tokens, tokens:], 0.0)
                 mix_rb = jnp.where(inclusive, gram[tokens:, :tokens], 0.0)
@@ -251,13 +264,13 @@
             index = 0
             for work in todo:
                 for side in work[5]:
-                    step.append(MM(inverse[index], jnp.where(pick, side[0], 0.0)))
+                    step.append(fine(inverse[index], jnp.where(pick, side[0], 0.0)))
                     index += 1
-            inverse = [now + MM(part, now) for now, part in zip(inverse, step)]
+            inverse = [now + fine(part, now) for now, part in zip(inverse, step)]
             size *= 2
 
         for pair, (at, left_r, val, ends, fade, sides) in enumerate(todo):
-            reads = [MM(inverse[2 * pair + head], sides[head][4]) for head in range(2)]
+            reads = [fine(inverse[2 * pair + head], sides[head][4]) for head in range(2)]
             both = reads[0] + reads[1]
             outs = once(
                 jnp.concatenate([sides[0][1], sides[1][1]], 1), jnp.concatenate(reads, 0)
@@ -294,7 +307,7 @@
             mixed = (lines + bonus).astype(BF16)
             mixed_ref[:, at] = mixed
             enc = (mixed.astype(F32) - center_ref[:, at]).astype(BF16)
-            placed = once(spread_ref[...], enc).astype(BF16)
+            placed = once(spread_s[...], enc).astype(BF16)
             stage_s[chunk, :, :, pair * LANES : (pair + 1) * LANES] = placed.reshape(
                 devices, pair_rows, LANES
             )
@@ -315,7 +328,7 @@
             for pair in range(PAIRS):
                 spot = chunk * PAIRS + pair
                 leave_s[chunk, pair] = (
-                    thrice(arrive_s[chunk, pair], trans_s[spot]) + own_s[spot]
+                    fine(arrive_s[chunk, pair], trans_s[spot]) + own_s[spot]
                 )
             onward(chunk).start()
 
@@ -382,10 +395,11 @@
         for block in range(STRIP // BLK):
             inside = slice(block * BLK, (block + 1) * BLK)
             at = slice(strip * STRIP + block * BLK, strip * STRIP + (block + 1) * BLK)
+            index = strip * (STRIP // BLK) + block
+            line = slice(index, index + 1)
             pre = pre_s[strip, :, inside] + peer_s[strip, :, inside].astype(F32)
-            code = jnp.maximum(pre + bias_ref[:, at], 0.0)
-            code = jnp.where(hit_ref[:, at] > 0.0, forced_ref[:, at], code)
-            index = strip * (STRIP // BLK) + block
+            code = jnp.maximum(pre + bias_ref[line, :], 0.0)
+            code = jnp.where(hit_ref[line, :] > 0.0, forced_ref[line, :], code)
             active = mask_s[:, :, index : index + 1].reshape(rows, 1).astype(F32)
             codes_s[:, at] = (code * active).astype(BF16)
 
@@ -404,7 +418,7 @@
         others(lambda other: part_copy(chunk, me, other).wait_recv())
         at = chunk_at(chunk)
         total = lax.dot_general(
-            gather_ref[...],
+            gather_s[...],
             back_s[chunk].reshape(rows, chunk_lanes),
             ROWS_COLS,
             preferred_element_type=F32,
@@ -429,16 +443,15 @@
         half_copy(strip).wait_send()
 
 
-MM = thrice
 STRIP = 512
 
 
-def whole(devices, rec, key, val, rate, learn, lines, spread, gather, tile_mask, latent_lines, table):
+def whole(devices, rec, key, val, rate, learn, lines, placing, tile_mask, latent_lines, table):
     tokens, width = rec.shape
     chunks = width // (PAIRS * LANES)
     pairs = width // LANES
     latents = table.shape[0]
-    rows = spread.shape[0]
+    rows = placing.shape[1]
     pair_rows = rows // devices
     strips = latents // STRIP
     shape = jax.ShapeDtypeStruct((tokens, width), BF16)
@@ -449,7 +462,7 @@
     return pl.pallas_call(
         functools.partial(whole_kernel, devices),
         out_shape=(shape, shape),
-        in_specs=[vmem] * 15 + [pl.BlockSpec(memory_space=pl.ANY)],
+        in_specs=[vmem] * 14 + [pl.BlockSpec(memory_space=pl.ANY)],
         out_specs=(vmem, vmem),
         scratch_shapes=[
             pltpu.VMEM((tokens, width), F32),
@@ -458,6 +471,8 @@
             pltpu.VMEM((pairs, ATTN_GROUP_DIM, LANES), F32),
             pltpu.VMEM((chunks, PAIRS, ATTN_GROUP_DIM, LANES), F32),
             pltpu.VMEM((chunks, PAIRS, ATTN_GROUP_DIM, LANES), F32),
+            pltpu.VMEM((rows, tokens), BF16),
+            pltpu.VMEM((tokens, rows), BF16),
             pltpu.VMEM((latents, width), BF16),
             blocks,
             blocks,
@@ -484,7 +499,7 @@
             collective_id=0, has_side_effects=True, vmem_limit_bytes=52 * 1024 * 1024
         ),
         name="whole",
-    )(rec, key, val, rate, learn, *lines, spread, gather, tile_mask, *latent_lines, table)
+    )(rec, key, val, rate, learn, *lines, placing, tile_mask, *latent_lines, table)
 
 
 def body(
@@ -517,21 +532,14 @@
     )
     ranks = jnp.sum(earlier.astype(jnp.int32), axis=1)
     slot_ids = owner_flat * capacity + ranks
-    dispatch = (
-        slot_ids[None, :] == lax.broadcasted_iota(jnp.int32, (ctx_count * capacity, 1), 0)
-    ).astype(jnp.float32)
-    tile_pick = (
-        lax.broadcasted_iota(jnp.int32, (tile_count, pair_count), 1) // slot_count
-        == lax.broadcasted_iota(jnp.int32, (tile_count, pair_count), 0)
-    ).astype(jnp.float32)
-    slot_tile = jnp.dot(dispatch, tile_pick.T)
-    each = jnp.eye(TILE, dtype=jnp.float32)
+    named = slot_ids[None, :] == lax.broadcasted_iota(jnp.int32, (ctx_count * capacity, 1), 0)
+    dispatch = named.astype(jnp.float32)
     rows = ctx_count * capacity * TILE
-    spread = (
-        (slot_tile[:, None, :, None] * each[None, :, None, :])
-        .reshape(rows, tok_rows)
-        .astype(jnp.bfloat16)
-    )
+    tile_of_pair = lax.broadcasted_iota(jnp.int32, (1, pair_count), 1) // slot_count
+    tile_of_slot = jnp.sum(jnp.where(named, tile_of_pair + 1, 0), axis=1) - 1
+    step = lax.broadcasted_iota(jnp.int32, (1, TILE), 1)
+    placing = jnp.where(tile_of_slot[:, None] < 0, -1, tile_of_slot[:, None] * TILE + step)
+    placing = placing.reshape(1, rows)
     tile_mask = jnp.dot(
         dispatch, holder_group_enabled.reshape(pair_count, blocks_own).astype(jnp.float32)
     )
@@ -539,8 +547,8 @@
     tile_mask = jnp.broadcast_to(tile_mask[:, None, :], (ctx_count * capacity, TILE, LANES))
     tile_mask = tile_mask.astype(jnp.bfloat16).reshape(ctx_count, capacity * TILE, LANES)
     within = lax.broadcasted_iota(jnp.int32, (blocks_own, BLK), 1)
-    hit = (within == fixed_feature_slot[:, None]).astype(jnp.float32).reshape(1, -1)
-    forced = jnp.broadcast_to(fixed_feature_amount[:, None], (blocks_own, BLK)).reshape(1, -1)
+    hit = (within == fixed_feature_slot[:, None]).astype(jnp.float32)
+    forced = jnp.broadcast_to(fixed_feature_amount[:, None], (blocks_own, BLK))
     lines = (group_layer_scaling, group_layer_offset, present_reward_factor, reconstruct_offset)
     return whole(
         ctx_count,
@@ -550,10 +558,9 @@
         forgetting_exponent,
         inline_adapt_factor,
         tuple(line[None] for line in lines),
-        spread,
-        spread.T,
+        placing,
         tile_mask,
-        (sparse_code_offset[None], hit, forced),
+        (sparse_code_offset.reshape(blocks_own, BLK), hit, forced),
         shared_dictionary_matrix,
     )
 

time: 155 us -> 158 us (1.019)
  local copies, waits for them, and re-layouts: 5.01 us -> 7.89 us
    unnamed x22 -> x16, local copies, waits for them, and re-layouts: 2.54 us -> 6.96 us
    convert_element_type x2 -> x0, local copies, waits for them, and re-layouts: 2.28 us -> none  [body(): spread = (slot_tile[:, None, :, None] * each[None, :, None, :]).reshape(r...]
where the time goes in v3:
time: 158 us
  Pallas kernels  147 us (93%)
  local copies, waits for them, and re-layouts  7.89 us (5%)
  other arithmetic  1.85 us (1%)
    pallas_call x1, Pallas kernels, whole(): pl.pallas_call(functools.partial(whole_kernel, devices), out_shape=(shape...  147 us
    unnamed x16, local copies, waits for them, and re-layouts  6.96 us

profile of v3, /device:TPU:1, one launch (start us, length us, event | category | flops | bytes accessed | tf_op | source)
XLA Modules:
  0.0 157.6 jit_solution(6891474591646888157)
XLA Ops:
  0.6 0.8 copy.21
  1.4 0.1 reshape.113
  1.5 0.2 convert_reduce_fusion
  1.7 0.1 select_reduce_fusion
  1.8 0.7 convert_element_type.18
  2.5 0.2 convolution_convert_fusion
  2.7 0.7 fusion.2.hit_ref
  3.4 0.7 broadcast_in_dim.61.forced_ref
  4.2 0.1 copy.23
  4.3 0.1 add_select_fusion
  4.4 0.1 select_n.31.placing_ref
  4.5 0.0 copy-start
  4.5 1.0 copy-done
  5.5 0.0 copy-start.1
  5.5 0.7 copy-done.1
  6.2 0.0 copy-start.2
  6.2 0.7 copy-done.2
  6.9 0.0 copy-start.3
  6.9 0.7 copy-done.3
  7.6 0.0 copy-start.4
  7.6 0.7 copy-done.4
  8.3 0.0 copy-start.5
  8.3 0.7 copy-done.5
  9.0 147.0 %whole.1 = (bf16[128,2048]{1,0:T(8,128)(2,1)S(1)}, bf16[128,2048]{1,0:T(8,128)(2,1)S(1)}) custom-call(bf16[128,2048]{1,0:T(8,128)(2,1)S(1)} %copy-done, bf16[128,2048]{1,0:T(8,128)(2,1)} %key_ref.1, bf16[128,2048]{1,0:T(8,128)(2,1)} %val_ref.1, bf16[128,2048]{1,0:T(8,128)(2,1)} %rate_ref.1, bf16[128,2048]{1,0:T(8,128)(2,1)} %learn_ref.1, ...), custom_call_target="tpu_custom_call" | custom-call | tf_op jit(solution)/shard_map/whole/pallas_call | solution.py:462
  156.0 0.8 copy.26
  156.8 0.8 copy.27
  (5 shorter events, 0.0 us)
Async XLA Ops:
  4.5 1.0 copy-start
  5.5 0.7 copy-start.1
  6.2 0.7 copy-start.2
  6.9 0.7 copy-start.3
  7.6 0.7 copy-start.4
  8.3 0.7 copy-start.5

commit v4 on v3

--- a/solution.py
+++ b/solution.py
@@ -30,15 +30,11 @@
     return high, (a - high.astype(F32)).astype(BF16)
 
 
-def fine(a, b):
+def thrice(a, b, dims=ROWS_COLS):
     a_high, a_low = split(a)
     b_high, b_low = split(b)
-    left = jnp.concatenate([a_high, a_low], 1)
-    if b.shape[1] == LANES:
-        right = jnp.concatenate([b_high, b_low], 1)
-        both = once(left, jnp.concatenate([right, right], 0))
-        return both[:, :LANES] + both[:, LANES:]
-    return once(left, jnp.concatenate([b_high, b_high], 0)) + once(a_high, b_low)
+    dot = functools.partial(lax.dot_general, dimension_numbers=dims, preferred_element_type=F32)
+    return dot(a_high, b_high) + (dot(a_high, b_low) + dot(a_low, b_high))
 
 
 def iota(shape, dim):
@@ -229,18 +225,13 @@
             right = jnp.concatenate([erase * undo, key * undo], 0)
             ends = jnp.concatenate([erase * fade_to_end, key * fade_to_end], 0)
             fade = jnp.exp(-total[tokens - 1 :, :])
-            right_high, right_low = split(right)
-            right_twice = jnp.concatenate([right_high, right_high], 1)
             sides = []
             for head in range(2):
                 mine = first if head == 0 else jnp.logical_not(first)
                 left = jnp.concatenate(
                     [jnp.where(mine, left_a, 0.0), jnp.where(mine, left_r, 0.0)], 0
                 )
-                left_high, left_low = split(left)
-                gram = once(
-                    jnp.concatenate([left_high, left_low], 1), right_twice, COLS_COLS
-                ) + once(left_high, right_low, COLS_COLS)
+                gram = once(left, right, COLS_COLS)
                 mix_ab = jnp.where(strict, gram[:tokens, :tokens], 0.0)
                 mix_ak = jnp.where(strict, gram[:tokens, tokens:], 0.0)
                 mix_rb = jnp.where(inclusive, gram[tokens:, :tokens], 0.0)
@@ -264,13 +255,13 @@
             index = 0
             for work in todo:
                 for side in work[5]:
-                    step.append(fine(inverse[index], jnp.where(pick, side[0], 0.0)))
+                    step.append(once(inverse[index], jnp.where(pick, side[0], 0.0)))
                     index += 1
-            inverse = [now + fine(part, now) for now, part in zip(inverse, step)]
+            inverse = [now + once(part, now) for now, part in zip(inverse, step)]
             size *= 2
 
         for pair, (at, left_r, val, ends, fade, sides) in enumerate(todo):
-            reads = [fine(inverse[2 * pair + head], sides[head][4]) for head in range(2)]
+            reads = [once(inverse[2 * pair + head], sides[head][4]) for head in range(2)]
             both = reads[0] + reads[1]
             outs = once(
                 jnp.concatenate([sides[0][1], sides[1][1]], 1), jnp.concatenate(reads, 0)
@@ -295,7 +286,7 @@
         )
         for pair in range(PAIRS):
             at = lanes_of(chunk, pair)
-            prior = arrive_s[chunk, pair]
+            prior = arrive_s[chunk, pair].astype(F32)
             prior = jnp.where(same_head, jnp.concatenate([prior, prior], 0), 0.0)
             wkv = local_s[:, at] + once(probe_s[:, at], prior, COLS_COLS)
             center = wkv - head_sum(wkv, first) * (1.0 / ATTN_GROUP_DIM)
@@ -317,7 +308,7 @@
     def chain(chunk):
         @pl.when(me == 0)
         def _():
-            arrive_s[chunk] = jnp.zeros(arrive_s.shape[1:], F32)
+            arrive_s[chunk] = jnp.zeros(arrive_s.shape[1:], BF16)
 
         @pl.when(me > 0)
         def _():
@@ -328,8 +319,8 @@
             for pair in range(PAIRS):
                 spot = chunk * PAIRS + pair
                 leave_s[chunk, pair] = (
-                    fine(arrive_s[chunk, pair], trans_s[spot]) + own_s[spot]
-                )
+                    thrice(arrive_s[chunk, pair].astype(F32), trans_s[spot]) + own_s[spot]
+                ).astype(BF16)
             onward(chunk).start()
 
         finish(chunk)
@@ -469,8 +460,8 @@
             pltpu.VMEM((tokens, width), F32),
             pltpu.VMEM((pairs, LANES, LANES), F32),
             pltpu.VMEM((pairs, ATTN_GROUP_DIM, LANES), F32),
-            pltpu.VMEM((chunks, PAIRS, ATTN_GROUP_DIM, LANES), F32),
-            pltpu.VMEM((chunks, PAIRS, ATTN_GROUP_DIM, LANES), F32),
+            pltpu.VMEM((chunks, PAIRS, ATTN_GROUP_DIM, LANES), BF16),
+            pltpu.VMEM((chunks, PAIRS, ATTN_GROUP_DIM, LANES), BF16),
             pltpu.VMEM((rows, tokens), BF16),
             pltpu.VMEM((tokens, rows), BF16),
             pltpu.VMEM((latents, width), BF16),

time: 158 us -> 151 us (0.956)
  Pallas kernels: 147 us -> 139 us
    pallas_call x1, Pallas kernels: 147 us -> 139 us  [whole(): pl.pallas_call(functools.partial(whole_kernel, devices), out_shape=(shape...]
where the time goes in v4:
time: 151 us; the launch traced here: 150 us
  Pallas kernels  139 us (92%)
  local copies, waits for them, and re-layouts  7.89 us (5%)
  other arithmetic  1.85 us (1%)
    pallas_call x1, Pallas kernels, whole(): pl.pallas_call(functools.partial(whole_kernel, devices), out_shape=(shape...  139 us
    unnamed x16, local copies, waits for them, and re-layouts  6.96 us

profile of v4, /device:TPU:1, one launch (start us, length us, event | category | flops | bytes accessed | tf_op | source)
XLA Modules:
  0.0 150.1 jit_solution(8919470046744859383)
XLA Ops:
  0.6 0.8 copy.21
  1.4 0.1 reshape.113
  1.5 0.2 convert_reduce_fusion
  1.7 0.1 select_reduce_fusion
  1.8 0.7 convert_element_type.18
  2.5 0.2 convolution_convert_fusion
  2.7 0.7 fusion.2.hit_ref
  3.4 0.7 broadcast_in_dim.61.forced_ref
  4.2 0.1 copy.23
  4.3 0.1 add_select_fusion
  4.4 0.1 select_n.31.placing_ref
  4.5 0.0 copy-start
  4.5 1.0 copy-done
  5.5 0.0 copy-start.1
  5.5 0.7 copy-done.1
  6.2 0.0 copy-start.2
  6.2 0.7 copy-done.2
  6.9 0.0 copy-start.3
  6.9 0.7 copy-done.3
  7.6 0.0 copy-start.4
  7.6 0.7 copy-done.4
  8.3 0.0 copy-start.5
  8.3 0.7 copy-done.5
  9.0 139.5 %whole.1 = (bf16[128,2048]{1,0:T(8,128)(2,1)S(1)}, bf16[128,2048]{1,0:T(8,128)(2,1)S(1)}) custom-call(bf16[128,2048]{1,0:T(8,128)(2,1)S(1)} %copy-done, bf16[128,2048]{1,0:T(8,128)(2,1)} %key_ref.1, bf16[128,2048]{1,0:T(8,128)(2,1)} %val_ref.1, bf16[128,2048]{1,0:T(8,128)(2,1)} %rate_ref.1, bf16[128,2048]{1,0:T(8,128)(2,1)} %learn_ref.1, ...), custom_call_target="tpu_custom_call" | custom-call | tf_op jit(solution)/shard_map/whole/pallas_call | solution.py:453
  148.5 0.8 copy.26
  149.3 0.8 copy.27
  (5 shorter events, 0.0 us)
Async XLA Ops:
  4.5 1.0 copy-start
  5.5 0.7 copy-start.1
  6.2 0.7 copy-start.2
  6.9 0.7 copy-start.3
  7.6 0.7 copy-start.4
  8.3 0.7 copy-start.5
